TPU v7x, 256 devices: a whole 4x4x8 slice. The times are simulated.
256 devices in a mesh: group: 2 (over z_lo), dp: 32 (over x, z_hi, core), mp: 4 (over y).
Axes of the slice: x: 4, y: 4, z: 8 (z_hi: 4, z_lo: 2; z = z_hi * 2 + z_lo), core: 2. Of those that a mesh axis runs over, the one named last changes fastest.
Arguments:
- states: bfloat16 [4096, 4096], P('dp', 'mp'), may hold values from -18 to 18
- neighbours: bfloat16 [128, 64, 4096], P('dp', None, 'mp'), may hold values from -18 to 18
- cotangent: bfloat16 [4096, 4096], P('dp', 'mp'), may hold values from -24 to 24
- span_of: int32 [128], P('dp'), may hold values from 0 to 63, as said below
- counts: int32 [32], P('dp'), may hold values from 2 to 4, as said below
- kv_weight: bfloat16 [2, 4096, 2, 4096], P('group', 'dp', None, 'mp'), may hold values from -1 to 1
- gains: float32 [2, 2, 4096], P('group', None, 'mp'), may hold values from 0.5 to 3
Outputs:
- results: float32 [2, 4096, 4096], P('group', 'dp', 'mp')
Inputs may be any that keep to these rules, and one draw needn't show every extreme that they name: `span_of`: slot j of dp shard d (row d * 4 + j) names a span of the same shard, d * 2 to d * 2 + 1. The live slots of a shard name its spans in order, every span by one or two slots. `counts`: the live slots of a shard lead its slots; some shard has all 4 live.
All inputs are finite; a program needn't handle non-finite values.
Results may differ from a plain program's by a relative error of at most 0.029.
Values may be sent and summed in bfloat16 or wider, within the bound.
A program may use at most 128 MiB of HBM per device.

v0:
```python
import jax
import jax.numpy as jnp
from jax import lax
from jax.sharding import PartitionSpec as P

HD = 128
HEAD_FEATURES = 4096
CH = 64


EPSILON = 1e-05
NEG_LARGE = -1e30


def passed_along(array, axis, by):
    length = lax.axis_size(axis)
    pairs = [(i, i + by) for i in range(length) if 0 <= i + by < length]
    return lax.ppermute(array, axis, pairs)


def masked_softmax(scores, key_mask):
    masked_scores = jnp.where(key_mask, scores, NEG_LARGE)
    highest = jnp.max(masked_scores, axis=-1, keepdims=True)
    raised = jnp.where(key_mask, jnp.exp(masked_scores - highest), 0.0)
    return raised / jnp.sum(raised, axis=-1, keepdims=True)


def attention_probs(queries, key_heads, key_mask, score_scale):
    scores = (
        jnp.einsum("qhd,khd->hqk", queries, key_heads, preferred_element_type=jnp.float32)
        * score_scale
    )
    return masked_softmax(scores, key_mask[None])


def attention_apply(rounded, values):
    return jnp.einsum("hqk,khd->qhd", rounded, values, preferred_element_type=jnp.float32)


def attend_back(grad_out, queries, values, attn_probs, rounded, score_scale):
    grad_values = jnp.einsum("hqk,qhd->khd", rounded, grad_out, preferred_element_type=jnp.float32)
    grad_probs = jnp.einsum("qhd,khd->hqk", grad_out, values, preferred_element_type=jnp.float32)
    grad_scores = attn_probs * (
        grad_probs - jnp.sum(grad_probs * attn_probs, axis=-1, keepdims=True)
    )
    grad_keys = score_scale * jnp.einsum(
        "hqk,qhd->khd", grad_scores, queries.astype(jnp.float32), preferred_element_type=jnp.float32
    )
    return (grad_keys, grad_values)


def project(rows_in, weight_rows):
    return jnp.einsum("nw,wkf->nkf", rows_in, weight_rows, preferred_element_type=jnp.float32)


def project_back(grad_pair, weight_rows):
    return jnp.einsum("nkf,wkf->nw", grad_pair, weight_rows, preferred_element_type=jnp.float32)


def per_device(states, neighbours, cotangent, span_of, counts, kv_weight, gains):
    group_index = lax.axis_index("group")
    dp_index = lax.axis_index("dp")
    tok_rows, features = states.shape
    slot_count, neigh_len = (neighbours.shape[0], neighbours.shape[1])
    row_count = slot_count * neigh_len
    heads_dev = features // HD
    spans_dev = tok_rows // CH
    score_scale = HD ** (-0.5)
    state_f = states.astype(jnp.float32)
    neighbour_float_rows = neighbours.reshape(row_count, features).astype(jnp.float32)
    state_total, neigh_total = lax.psum(
        (
            jnp.sum(state_f * state_f, axis=1),
            jnp.sum(neighbour_float_rows * neighbour_float_rows, axis=1),
        ),
        "mp",
    )
    inv_state = lax.rsqrt(state_total / HEAD_FEATURES + EPSILON)
    inv_neigh = lax.rsqrt(neigh_total / HEAD_FEATURES + EPSILON)
    gain_first = gains[0, 0]
    gain_second = gains[0, 1]
    local_span = span_of - dp_index * spans_dev
    row_span = jnp.repeat(local_span, neigh_len)
    live_rows = jnp.repeat(jnp.arange(slot_count) < counts[0], neigh_len)
    token_span = jnp.arange(tok_rows) // CH
    enc_mask = row_span[:, None] == token_span[None, :]
    enc_queries = (
        (neighbour_float_rows * inv_neigh[:, None] * gain_second)
        .astype(jnp.bfloat16)
        .reshape(row_count, heads_dev, HD)
    )
    whole_rows = lax.all_gather(kv_weight[0], "dp", axis=0, tiled=True)
    normed_state = (state_f * inv_state[:, None] * gain_first).astype(jnp.bfloat16)
    full_state = lax.all_gather(normed_state, "mp", axis=1, tiled=True)
    state_terms = project(full_state, whole_rows)
    state_kv = state_terms.astype(jnp.bfloat16)
    enc_probs = attention_probs(
        enc_queries, state_kv[:, 0].reshape(tok_rows, heads_dev, HD), enc_mask, score_scale
    )
    enc_output = attention_apply(
        enc_probs.astype(jnp.bfloat16), state_kv[:, 1].reshape(tok_rows, heads_dev, HD)
    )
    encoder_output = (
        (neighbour_float_rows + enc_output.reshape(row_count, features))
        .astype(jnp.bfloat16)
        .reshape(slot_count, neigh_len, features)
    )
    arrived = passed_along(encoder_output, "group", -1)
    arrived_f = arrived.reshape(row_count, features).astype(jnp.float32)
    enc_total = lax.psum(jnp.sum(arrived_f * arrived_f, axis=1), "mp")
    inv_enc = lax.rsqrt(enc_total / HEAD_FEATURES + EPSILON)
    normed_enc = (arrived_f * inv_enc[:, None] * gain_second).astype(jnp.bfloat16)
    full_enc = lax.all_gather(normed_enc, "mp", axis=1, tiled=True)
    neigh_terms = project(full_enc, whole_rows)
    neighbour_key_value = neigh_terms.astype(jnp.bfloat16)
    dec_queries = normed_state.reshape(tok_rows, heads_dev, HD)
    dec_values = neighbour_key_value[:, 1].reshape(row_count, heads_dev, HD)
    dec_mask = (token_span[:, None] == row_span[None, :]) & live_rows[None, :]
    dec_probs = attention_probs(
        dec_queries,
        neighbour_key_value[:, 0].reshape(row_count, heads_dev, HD),
        dec_mask,
        score_scale,
    )
    dec_rounded = dec_probs.astype(jnp.bfloat16)
    mixed_out = state_f + attention_apply(dec_rounded, dec_values).reshape(tok_rows, features)
    dec_grad_keys, dec_grad_values = attend_back(
        cotangent.reshape(tok_rows, heads_dev, HD),
        dec_queries,
        dec_values,
        dec_probs,
        dec_rounded,
        score_scale,
    )
    dec_grad_pair = jnp.stack(
        [dec_grad_keys.reshape(row_count, features), dec_grad_values.reshape(row_count, features)],
        axis=1,
    ).astype(jnp.bfloat16)
    neigh_partial = project_back(dec_grad_pair, whole_rows)
    grad_normed = lax.psum_scatter(
        neigh_partial.astype(jnp.bfloat16), "mp", scatter_dimension=1, tiled=True
    ).astype(jnp.float32)
    row_dot = lax.psum(jnp.sum(gain_second * arrived_f * grad_normed, axis=1), "mp")
    factor = inv_enc**3 * row_dot / HEAD_FEATURES
    grad_enc = inv_enc[:, None] * gain_second * grad_normed - arrived_f * factor[:, None]
    grad_encoded = grad_enc.astype(jnp.bfloat16).reshape(slot_count, neigh_len, features)
    returned = passed_along(grad_encoded, "group", 1)
    state_values = state_kv[:, 1].reshape(tok_rows, heads_dev, HD)
    grad_out = returned.reshape(row_count, heads_dev, HD)
    enc_grad_keys, enc_grad_values = attend_back(
        grad_out, enc_queries, state_values, enc_probs, enc_probs.astype(jnp.bfloat16), score_scale
    )
    enc_grad_pair = jnp.stack(
        [enc_grad_keys.reshape(tok_rows, features), enc_grad_values.reshape(tok_rows, features)],
        axis=1,
    ).astype(jnp.bfloat16)
    state_partial = project_back(enc_grad_pair, whole_rows)
    grad_input = lax.psum_scatter(
        state_partial.astype(jnp.bfloat16), "mp", scatter_dimension=1, tiled=True
    ).astype(jnp.float32)
    state_dot = lax.psum(jnp.sum(gain_first * state_f * grad_input, axis=1), "mp")
    grad_states = (
        inv_state[:, None] * gain_first * grad_input
        - state_f * (inv_state**3 * state_dot / HEAD_FEATURES)[:, None]
    )
    return jnp.where(group_index == 0, mixed_out, grad_states)[None]


def solution(mesh):
    return jax.shard_map(
        per_device,
        mesh=mesh,
        in_specs=(
            P("dp", "mp"),
            P("dp", None, "mp"),
            P("dp", "mp"),
            P("dp"),
            P("dp"),
            P("group", "dp", None, "mp"),
            P("group", None, "mp"),
        ),
        out_specs=P("group", "dp", "mp"),
        check_vma=False,
    )
```

profile of v0, /device:TPU:2, one launch (start us, length us, event | category | flops | bytes accessed | tf_op | source)
XLA Modules:
  0.0 404.7 jit_solution(4654584966249461103)
XLA Ops:
  9.7 10.7 %all-reduce = (f32[128]{0:T(128)S(1)}, f32[256]{0:T(256)S(1)}) all-reduce(f32[128]{0:T(128)S(1)} %fusion.59, f32[256]{0:T(256)S(1)} %reduce_sum.87), channel_id=1, replica_groups=mesh['group'=2,'dp'=32,'mp'=4] {'mp'}, use_global_device_ids=true, to_apply=%region_1.0 | all-reduce | flops 384 | bytes 3072 | tf_op jit(solution)/shard_map/psum | solution.py:71
  26.9 22.7 %all-gather.5.cloned.1.call-done = bf16[128,4096]{1,0:T(8,128)(2,1)} async-done(((bf16[128,1024]{1,0:T(8,128)(2,1)}), bf16[128,4096]{1,0:T(8,128)(2,1)}) %all-gather.5.cloned.1.call-update) | async-done | bytes 1048592 | tf_op jit(solution)/shard_map/all_gather | solution.py:94
  49.6 111.4 %all-gather.9.cloned.1.call-done = bf16[1,4096,2,1024]{3,1,2,0:T(8,128)(2,1)} async-done(((bf16[1,128,2,1024]{3,1,2,0:T(8,128)(2,1)}), bf16[1,4096,2,1024]{3,1,2,0:T(8,128)(2,1)}) %all-gather.9.cloned.1.call-update) | async-done | bytes 16777232 | tf_op jit(solution)/shard_map/all_gather | solution.py:92
  161.0 8.4 %fusion.36 = bf16[128,2,1024]{2,0,1:T(8,128)(2,1)S(1)} fusion(bf16[1,4096,2,1024]{3,1,2,0:T(8,128)(2,1)} %all-gather.9.cloned.1.call-done, bf16[128,4096]{1,0:T(8,128)(2,1)} %all-gather.5.cloned.1.call-done), kind=kOutput, calls=%fused_computation.31 | convolution fusion | flops 2147745792 | bytes 18350080 | tf_op jit(solution)/shard_map/nw,wkf->nkf/dot_general | solution.py:53
  172.8 2.6 copy.38
  175.3 2.4 reshape.158
  180.4 23.7 %collective-permute-done = bf16[4,64,1024]{2,1,0:T(8,128)(2,1)S(1)} collective-permute-done((bf16[4,64,1024]{2,1,0:T(8,128)(2,1)S(1)}, bf16[4,64,1024]{2,1,0:T(8,128)(2,1)S(1)}, u32[]{:S(2)}, u32[]{:S(2)}) %collective-permute-start) | collective-permute-done | bytes 524320 | tf_op jit(solution)/shard_map/ppermute | solution.py:18
  204.4 10.9 %psum.37 = f32[256]{0:T(256)S(1)} all-reduce(f32[256]{0:T(256)S(1)} %reduce_sum.90), channel_id=1, replica_groups=mesh['group'=2,'dp'=32,'mp'=4] {'mp'}, use_global_device_ids=true, to_apply=%region_7.8 | all-reduce | flops 256 | bytes 2048 | tf_op jit(solution)/shard_map/psum | solution.py:110
  219.1 27.4 %all-gather.7.cloned.1.call-done = bf16[256,4096]{1,0:T(8,128)(2,1)} async-done(((bf16[256,1024]{1,0:T(8,128)(2,1)}), bf16[256,4096]{1,0:T(8,128)(2,1)}) %all-gather.7.cloned.1.call-update) | async-done | bytes 2097168 | tf_op jit(solution)/shard_map/all_gather | solution.py:113
  246.5 10.9 %fusion.23 = bf16[256,2,1024]{2,0,1:T(8,128)(2,1)S(1)} fusion(bf16[1,4096,2,1024]{3,1,2,0:T(8,128)(2,1)} %all-gather.9.cloned.1.call-done, bf16[256,4096]{1,0:T(8,128)(2,1)} %all-gather.7.cloned.1.call-done), kind=kOutput, calls=%fused_computation.15 | convolution fusion | flops 4295491584 | bytes 19922944 | tf_op jit(solution)/shard_map/nw,wkf->nkf/dot_general | solution.py:53
  258.5 2.7 fusion.94
  261.2 2.5 convolution_convert_fusion
  265.5 2.7 fusion.39
  268.2 2.0 copy.48
  270.2 2.1 copy.49
  272.3 12.0 %fusion.13 = bf16[256,4096]{1,0:T(8,128)(2,1)} fusion(bf16[1,4096,2,1024]{3,1,2,0:T(8,128)(2,1)} %all-gather.9.cloned.1.call-done, bf16[256,1,1024]{2,0,1:T(8,128)(2,1)} %copy.49, bf16[256,1,1024]{2,0,1:T(8,128)(2,1)} %copy.48), kind=kOutput, calls=%fused_computation.11 | convolution fusion | flops 4296540160 | bytes 19922944 | tf_op jit(solution)/shard_map/nkf,wkf->nw/dot_general | solution.py:57
  284.3 32.4 %reduce-scatter.3.cloned.1.call-done = bf16[256,1024]{1,0:T(8,128)(2,1)} async-done(((bf16[256,4096]{1,0:T(8,128)(2,1)}), bf16[256,1024]{1,0:T(8,128)(2,1)}) %reduce-scatter.3.cloned.1.call-update) | async-done | bytes 524304 | tf_op jit(solution)/shard_map/reduce_scatter | solution.py:140
  318.0 8.6 %psum.38 = f32[256]{0:T(256)S(1)} all-reduce(f32[256]{0:T(256)S(1)} %fusion.43), channel_id=1, replica_groups=mesh['group'=2,'dp'=32,'mp'=4] {'mp'}, use_global_device_ids=true, to_apply=%region_13.14 | all-reduce | flops 256 | bytes 2048 | tf_op jit(solution)/shard_map/psum | solution.py:143
  327.9 3.7 collective-permute-start.1
  331.7 9.0 %collective-permute-done.1 = bf16[4,64,1024]{2,1,0:T(8,128)(2,1)S(1)} collective-permute-done((bf16[4,64,1024]{2,1,0:T(8,128)(2,1)S(1)}, bf16[4,64,1024]{2,1,0:T(8,128)(2,1)S(1)}, u32[]{:S(2)}, u32[]{:S(2)}) %collective-permute-start.1) | collective-permute-done | bytes 524320 | tf_op jit(solution)/shard_map/ppermute | solution.py:18
  343.4 2.7 multiply_reduce_fusion
  348.3 12.4 %fusion.19 = bf16[128,4096]{1,0:T(8,128)(2,1)} fusion(bf16[1,4096,2,1024]{3,1,2,0:T(8,128)(2,1)} %all-gather.9.cloned.1.call-done, bf16[128,1,1024]{2,0,1:T(8,128)(2,1)S(1)} %copy.56, bf16[128,1,1024]{2,0,1:T(8,128)(2,1)S(1)} %copy.55), kind=kOutput, calls=%fused_computation.13 | convolution fusion | flops 2148270080 | bytes 18350080 | tf_op jit(solution)/shard_map/nkf,wkf->nw/dot_general | solution.py:57
  361.4 25.1 %reduce-scatter.5.cloned.1.call-done = bf16[128,1024]{1,0:T(8,128)(2,1)} async-done(((bf16[128,4096]{1,0:T(8,128)(2,1)}), bf16[128,1024]{1,0:T(8,128)(2,1)}) %reduce-scatter.5.cloned.1.call-update) | async-done | bytes 262160 | tf_op jit(solution)/shard_map/reduce_scatter | solution.py:158
  387.7 8.5 %psum.39 = f32[128]{0:T(128)S(1)} all-reduce(f32[128]{0:T(128)S(1)} %fusion.58), channel_id=1, replica_groups=mesh['group'=2,'dp'=32,'mp'=4] {'mp'}, use_global_device_ids=true, to_apply=%region_17.18 | all-reduce | flops 128 | bytes 1024 | tf_op jit(solution)/shard_map/psum | solution.py:161
  (71 shorter events, 33.3 us)
Async XLA Ops:
  6.5 43.1 %all-gather.5.cloned.1.call-start = ((), (), s32[]{:S(2)}) async-start(), calls=%async_computation.2 | async-start | bytes 1310720 | tf_op jit(solution)/shard_map/all_gather | solution.py:94
  22.3 138.7 %all-gather.9.cloned.1.call-start = ((), (), s32[]{:S(2)}) async-start(), calls=%async_computation.6 | async-start | bytes 17301504 | tf_op jit(solution)/shard_map/all_gather | solution.py:92
  24.3 222.2 %all-gather.7.cloned.1.call-start = ((), (), s32[]{:S(2)}) async-start(), calls=%async_computation.3 | async-start | bytes 2621440 | tf_op jit(solution)/shard_map/all_gather | solution.py:113
  26.9 150.9 %copy-start = (bf16[4,64,1024]{2,1,0:T(8,128)(2,1)S(1)}, bf16[4,64,1024]{2,1,0:T(8,128)(2,1)}, u32[]{:S(2)}) copy-start(bf16[4,64,1024]{2,1,0:T(8,128)(2,1)} %param.8) | copy-start | bytes 1572868
  26.9 189.7 %copy-start.2 = (bf16[128,1024]{1,0:T(8,128)(2,1)S(1)}, bf16[128,1024]{1,0:T(8,128)(2,1)}, u32[]{:S(2)}) copy-start(bf16[128,1024]{1,0:T(8,128)(2,1)} %fusion.61) | copy-start | bytes 786436
  26.9 191.3 %copy-start.3 = (bf16[128,1024]{1,0:T(8,128)(2,1)S(1)}, bf16[128,1024]{1,0:T(8,128)(2,1)}, u32[]{:S(2)}) copy-start(bf16[128,1024]{1,0:T(8,128)(2,1)} %param.9) | copy-start | bytes 786436
  179.1 25.0 %collective-permute-start = (bf16[4,64,1024]{2,1,0:T(8,128)(2,1)S(1)}, bf16[4,64,1024]{2,1,0:T(8,128)(2,1)S(1)}, u32[]{:S(2)}, u32[]{:S(2)}) collective-permute-start(bf16[4,64,1024]{2,1,0:T(8,128)(2,1)S(1)} %add_convert_fusion), channel_id=1, source_target_pairs={{128,0},{129,1},{130,2},{131,3},{132,4},{133,5},{134,6},{135,7},{1... | collective-permute-start | bytes 1572872 | tf_op jit(solution)/shard_map/ppermute | solution.py:18
  216.3 100.4 %reduce-scatter.3.cloned.1.call-start = ((), (), s32[]{:S(2)}) async-start(), calls=%async_computation.4 | async-start | bytes 2621440 | tf_op jit(solution)/shard_map/reduce_scatter | solution.py:140
  284.3 102.3 %reduce-scatter.5.cloned.1.call-start = ((), (), s32[]{:S(2)}) async-start(), calls=%async_computation.5 | async-start | bytes 1310720 | tf_op jit(solution)/shard_map/reduce_scatter | solution.py:158
  327.9 12.7 %collective-permute-start.1 = (bf16[4,64,1024]{2,1,0:T(8,128)(2,1)S(1)}, bf16[4,64,1024]{2,1,0:T(8,128)(2,1)S(1)}, u32[]{:S(2)}, u32[]{:S(2)}) collective-permute-start(bf16[4,64,1024]{2,1,0:T(8,128)(2,1)S(1)} %bitcast.123), channel_id=1, source_target_pairs={{0,128},{1,129},{2,130},{3,131},{4,132},{5,133},{6,134},{7,135},{8... | collective-permute-start | bytes 1572872 | tf_op jit(solution)/shard_map/ppermute | solution.py:18
  346.0 40.5 %copy-start.1 = (bf16[128,1024]{1,0:T(8,128)(2,1)S(1)}, bf16[128,1024]{1,0:T(8,128)(2,1)}, u32[]{:S(2)}) copy-start(bf16[128,1024]{1,0:T(8,128)(2,1)} %param.7) | copy-start | bytes 786436
  348.0 12.8 %copy-start.4 = (f32[8,128,256]{2,1,0:T(8,128)S(1)}, f32[8,128,256]{2,1,0:T(8,128)}, u32[]{:S(2)}) copy-start(f32[8,128,256]{2,1,0:T(8,128)} %get-tuple-element.16) | copy-start | bytes 3145732
Sparse Core Ops, SparseCore 0:
  22.4 27.1 all-gather.4
  52.3 108.6 all-gather.8
  216.4 30.0 all-gather.6
  284.4 32.2 reduce-scatter.2
  360.8 25.6 reduce-scatter.4
where the time goes:
time: 406 us; the launch traced here: 405 us
  waiting for transfers between devices  252 us (62%)
  matrix products  61.9 us (15%)
  blocking collectives  38.7 us (10%)
  local copies, waits for them, and re-layouts  18.4 us (5%)
  other arithmetic  14.5 us (4%)
  between operations  14.1 us (3%)
  starting transfers between devices  5.35 us (1%)
    all_gather x1, waiting for transfers between devices, per_device(): whole_rows = lax.all_gather(kv_weight[0], 'dp', axis=0, tiled=True)  111 us
    ppermute x2, waiting for transfers between devices, passed_along(): return lax.ppermute(array, axis, pairs)  32.7 us
    reduce_scatter x1, waiting for transfers between devices, per_device(): lax.psum_scatter(neigh_partial.astype(jnp.bfloat16), 'mp', scatter_dimens...  32.4 us
    all_gather x1, waiting for transfers between devices, per_device(): full_enc = lax.all_gather(normed_enc, 'mp', axis=1, tiled=True)  27.4 us
    reduce_scatter x1, waiting for transfers between devices, per_device(): lax.psum_scatter(state_partial.astype(jnp.bfloat16), 'mp', scatter_dimens...  25.1 us
    dot_general x2, matrix products, project_back(): jnp.einsum('nkf,wkf->nw', grad_pair, weight_rows, preferred_element_type=...  24.4 us
    all_gather x1, waiting for transfers between devices, per_device(): full_state = lax.all_gather(normed_state, 'mp', axis=1, tiled=True)  22.7 us
    dot_general x2, matrix products, project(): jnp.einsum('nw,wkf->nkf', rows_in, weight_rows, preferred_element_type=jn...  19.3 us
  transfers between devices with their start and end apart: 7, of which 7 were waited for; matrix products, arithmetic and copies ran while one was open for 2% of the time, Pallas kernels for 0%

commit v1 on v0

v1 whole, which is shorter than its diff:
```python
import functools

import jax
import jax.numpy as jnp
from jax import lax
from jax.experimental import pallas as pl
from jax.experimental.pallas import tpu as pltpu
from jax.sharding import PartitionSpec as P

HD = 128
FEATURES = 4096
CH = 64
EPSILON = 1e-05
NEG_LARGE = -1e30
TOK = 128
ROWS = 256
COLS = 1024
HALF = 512
HEADS = 4
SCALE = HD ** (-0.5)
BF = jnp.bfloat16
F32 = jnp.float32
SEMS = 224


def nt(a, b):
    return lax.dot_general(a, b, (((1,), (1,)), ((), ())), preferred_element_type=F32)


def nn(a, b):
    return lax.dot_general(a, b, (((1,), (0,)), ((), ())), preferred_element_type=F32)


def tn(a, b):
    return lax.dot_general(a, b, (((0,), (0,)), ((), ())), preferred_element_type=F32)


class Comm:
    def __init__(self, ssem, rsem):
        self.ssem, self.rsem = ssem, rsem
        self.used, self.sent = 0, []

    def alloc(self, count):
        base = self.used
        self.used += count
        assert self.used <= SEMS
        return base

    def copy(self, slot, src, dst, dev):
        return pltpu.make_async_remote_copy(
            src_ref=src,
            dst_ref=dst,
            send_sem=self.ssem.at[slot],
            recv_sem=self.rsem.at[slot],
            device_id=dev,
            device_id_type=pl.DeviceIdType.MESH,
        )

    def send(self, slot, src, dst, dev):
        copy = self.copy(slot, src, dst, dev)
        copy.start()
        self.sent.append(copy)

    def recv(self, slot, dst, dev):
        self.copy(slot, dst, dst, dev).wait_recv()

    def drain(self):
        for copy in self.sent:
            copy.wait_send()


class Ring:
    def __init__(self, comm, half, plus, minus):
        self.comm, self.half, self.plus, self.minus = comm, half, plus, minus
        self.base = comm.alloc(6)

    def start(self):
        for slot, k, dev in ((0, 0, self.plus), (2, 1, self.minus), (1, 1, self.plus), (3, 0, self.minus)):
            self.comm.send(self.base + slot, self.half(0, k), self.half(0, k), dev)

    def forward(self):
        self.comm.recv(self.base, self.half(-1, 0), self.minus)
        self.comm.send(self.base + 4, self.half(-1, 0), self.half(-1, 0), self.plus)
        self.comm.recv(self.base + 2, self.half(1, 1), self.plus)
        self.comm.send(self.base + 5, self.half(1, 1), self.half(1, 1), self.minus)

    def near(self):
        self.comm.recv(self.base + 1, self.half(-1, 1), self.minus)
        self.comm.recv(self.base + 3, self.half(1, 0), self.plus)

    def far(self):
        self.comm.recv(self.base + 4, self.half(2, 0), self.minus)
        self.comm.recv(self.base + 5, self.half(2, 1), self.plus)


class Scatter:
    def __init__(self, comm, part, bufs, plus, minus, rows):
        self.comm, self.part, self.plus, self.minus, self.n = comm, part, plus, minus, rows // 2
        self.from_minus, self.from_plus, self.last_minus, self.last_plus = bufs
        self.base = comm.alloc(6)

    def lo(self, ref):
        return ref.at[pl.ds(0, self.n), :]

    def hi(self, ref):
        return ref.at[pl.ds(self.n, self.n), :]

    def first(self):
        self.comm.send(self.base, self.lo(self.part(2)), self.from_minus, self.plus)
        self.comm.send(self.base + 1, self.hi(self.part(2)), self.from_plus, self.minus)

    def second(self):
        self.comm.send(self.base + 2, self.hi(self.part(1)), self.hi(self.last_minus), self.plus)
        self.comm.send(self.base + 3, self.lo(self.part(-1)), self.lo(self.last_plus), self.minus)

    def third(self):
        self.comm.recv(self.base, self.from_minus, self.minus)
        a = self.lo(self.part(1))
        a[...] = (a[...].astype(F32) + self.from_minus[...].astype(F32)).astype(BF)
        self.comm.send(self.base + 4, a, self.lo(self.last_minus), self.plus)
        self.comm.recv(self.base + 1, self.from_plus, self.plus)
        b = self.hi(self.part(-1))
        b[...] = (b[...].astype(F32) + self.from_plus[...].astype(F32)).astype(BF)
        self.comm.send(self.base + 5, b, self.hi(self.last_plus), self.minus)

    def total(self):
        self.comm.recv(self.base + 2, self.hi(self.last_minus), self.minus)
        self.comm.recv(self.base + 3, self.lo(self.last_plus), self.plus)
        self.comm.recv(self.base + 4, self.lo(self.last_minus), self.minus)
        self.comm.recv(self.base + 5, self.hi(self.last_plus), self.plus)
        return (
            self.part(0)[...].astype(F32)
            + self.last_minus[...].astype(F32)
            + self.last_plus[...].astype(F32)
        )


def as_row(col):
    return jnp.transpose(jnp.broadcast_to(col, (col.shape[0], 128)))[0:8, :]


def as_col(row):
    return jnp.transpose(jnp.broadcast_to(row[0:1, :], (128, row.shape[1])))[:, 0:1]


def kernel(
    wsrc, states, neigh, cot, span, counts, gains, out,
    w1, w0, sx, xn, gb, ns, eb, en, acc1, skv, qe, pe, acc2, nkv, dq, g2, pb, rba, rbb, r3, ysum,
    g1, pb1, rca, rcb, t3, ysum1, rd, rdp, rd1, rdp1, mxs, mxr,
    ssem, rsem, lsem,
):
    g = lax.axis_index("group")
    d = lax.axis_index("dp")
    y = lax.axis_index("mp")
    x, zh, c = d // 8, (d // 2) % 4, d % 2
    comm = Comm(ssem, rsem)

    def mod4(v):
        return (v + 4) % 4

    def at_x(r):
        return {"dp": mod4(x + r) * 8 + zh * 2 + c}

    def at_z(r):
        return {"dp": x * 8 + mod4(zh + r) * 2 + c}

    def at_y(r):
        return {"mp": mod4(y + r)}

    partner = {"group": 1 - g}
    sibling = {"dp": d + 1 - 2 * c}
    xp, xm, zp, zm, yp, ym, y2 = at_x(1), at_x(-1), at_z(1), at_z(-1), at_y(1), at_y(-1), at_y(2)

    barrier = pltpu.get_barrier_semaphore()
    peers = (partner, sibling, xp, xm, zp, zm, yp, ym, y2)
    for dev in peers:
        pl.semaphore_signal(barrier, inc=1, device_id=dev, device_id_type=pl.DeviceIdType.MESH)
    pl.semaphore_wait(barrier, len(peers))

    def wrow(rx, rz, core):
        return pl.multiple_of((mod4(x + rx) * 8 + mod4(zh + rz) * 2 + core) * TOK, TOK)

    own_rows = pl.ds(wrow(0, 0, c), TOK)

    def exchange(w, owner):
        local = pltpu.make_async_copy(wsrc.at[g], w.at[own_rows, :], lsem.at[owner])
        away = comm.copy(comm.alloc(1), wsrc.at[1 - g], w.at[own_rows, :], partner)

        @pl.when(g == owner)
        def _():
            away.start()
            local.start()

        def ready():
            @pl.when(g == owner)
            def _():
                local.wait()

            @pl.when(g != owner)
            def _():
                away.wait_recv()

        def done():
            @pl.when(g == owner)
            def _():
                away.wait_send()

        return ready, done

    ready1, done1 = exchange(w1, 1)
    ready0, done0 = exchange(w0, 0)

    def gather(w, ready, state):
        def block(rx, rz, core):
            return w.at[pl.ds(wrow(rx, rz, core), TOK), :]

        def half(rx, rz, k):
            return w.at[pl.ds(pl.multiple_of(wrow(rx, rz, c) + k * 64, 64), 64), :]

        sib_base = comm.alloc(16)

        def sib(rx, rz):
            comm.send(sib_base + (rx % 4) * 4 + rz % 4, block(rx, rz, c), block(rx, rz, c), sibling)

        def sib_wait(rz):
            for rx in range(4):
                comm.recv(sib_base + rx * 4 + rz % 4, block(rx, rz, 1 - c), sibling)

        state["wait"] = sib_wait
        zr = Ring(comm, lambda r, k: half(0, r, k), zp, zm)
        xr = {
            rz: Ring(comm, functools.partial(lambda rz, r, k: half(r, rz, k), rz), xp, xm)
            for rz in (0, -1, 1, 2)
        }
        ready()
        zr.start()
        yield
        xr[0].start()
        sib(0, 0)
        yield
        zr.forward()
        xr[0].forward()
        yield
        zr.near()
        for rz in (-1, 1):
            xr[rz].start()
            sib(0, rz)
        yield
        xr[0].near()
        sib(-1, 0)
        sib(1, 0)
        xr[0].far()
        sib(2, 0)
        yield
        zr.far()
        xr[2].start()
        sib(0, 2)
        yield
        xr[-1].forward()
        xr[1].forward()
        yield
        for rz in (-1, 1):
            xr[rz].near()
            sib(-1, rz)
            sib(1, rz)
        xr[2].forward()
        yield
        for rz in (-1, 1):
            xr[rz].far()
            sib(2, rz)
        yield
        xr[2].near()
        sib(-1, 2)
        sib(1, 2)
        xr[2].far()
        sib(2, 2)
        yield

    st1, st0 = {}, {}
    run1, run0 = gather(w1, ready1, st1), gather(w0, ready0, st0)

    def shalf(r, k):
        return sx.at[mod4(y + r), pl.ds(k * 64, 64), :]

    sx[y] = states[...]
    even = lax.broadcasted_iota(jnp.int32, (8, COLS), 0) % 2 == 0
    gb[y, g] = jnp.where(even, gains[0:1, :], gains[1:2, :])
    sring = Ring(comm, shalf, yp, ym)
    sring.start()
    gain_slot = comm.alloc(4)
    comm.send(gain_slot, gb.at[y, g], gb.at[y, g], partner)
    next(run1)
    next(run1)

    def small_start(buf, base):
        for i, (r, dev) in enumerate(((1, yp), (-1, ym), (2, y2))):
            comm.send(base + i, buf.at[y], buf.at[y], dev)

    def small_wait(buf, base):
        for i, (r, dev) in enumerate(((-1, ym), (1, yp), (2, y2))):
            comm.recv(base + i, buf.at[mod4(y + r)], dev)

    nf = neigh[...].astype(F32)
    ns[y] = as_row(jnp.sum(nf * nf, axis=1, keepdims=True))
    ns_base = comm.alloc(3)
    small_start(ns, ns_base)
    comm.recv(gain_slot, gb.at[y, 1 - g], partner)
    small_start(gb, gain_slot + 1)
    sring.forward()
    next(run1)
    sring.near()
    sring.far()
    small_wait(ns, ns_base)
    small_wait(gb, gain_slot + 1)

    mine = pl.ds(pl.multiple_of(g * HALF, HALF), HALF)
    sums = jnp.zeros((TOK, 1), F32)
    for i in range(4):
        v = sx[i].astype(F32)
        sums = sums + jnp.sum(v * v, axis=1, keepdims=True)
    inv_state = lax.rsqrt(sums / FEATURES + EPSILON)

    def norm_states(i, carry):
        xn[i] = (sx[i].astype(F32) * inv_state * gb[i, 1, 0:1, :]).astype(BF)
        return carry

    lax.fori_loop(0, 4, norm_states, 0)
    dq[...] = (states[:, mine].astype(F32) * inv_state * gb[y, 0, 0:1, mine]).astype(BF)
    inv_neigh = as_col(lax.rsqrt((ns[0] + ns[1] + ns[2] + ns[3]) / FEATURES + EPSILON))
    qe[...] = (neigh[:, mine].astype(F32) * inv_neigh * gb[y, 1, 1:2, mine]).astype(BF)

    def project_states(rz, first):
        st1["wait"](rz)
        z = mod4(zh + rz)

        def step(i, carry):
            rows = pl.ds(pl.multiple_of((i * 4 + z) * 256, 256), 256)
            part = nn(xn[i, :, pl.ds(pl.multiple_of(z * 256, 256), 256)], w1[rows, :])
            acc1[...] += part
            return carry

        if first:
            acc1[...] = jnp.zeros_like(acc1)
        lax.fori_loop(0, 4, step, 0)

    next(run1)
    next(run1)
    next(run1)
    next(run0)
    project_states(0, True)
    next(run1)
    next(run1)
    next(run1)
    next(run0)
    project_states(-1, False)
    project_states(1, False)
    next(run1)
    project_states(2, False)
    skv[...] = acc1[...].astype(BF)

    base_span = d * 2

    def spans_of(slot):
        spans = [span[i] - base_span for i in range(4)]
        return jnp.where(
            slot == 0, spans[0], jnp.where(slot == 1, spans[1], jnp.where(slot == 2, spans[2], spans[3]))
        )

    def iota(shape, axis):
        return lax.broadcasted_iota(jnp.int32, shape, axis)

    enc_mask = spans_of(iota((ROWS, TOK), 0) >> 6) == (iota((ROWS, TOK), 1) >> 6)
    slots_t = iota((TOK, ROWS), 1) >> 6
    dec_mask = (spans_of(slots_t) == (iota((TOK, ROWS), 0) >> 6)) & (slots_t < counts[0])

    def softmax(scores, mask):
        scores = jnp.where(mask, scores * SCALE, NEG_LARGE)
        top = jnp.max(scores, axis=-1, keepdims=True)
        raised = jnp.where(mask, jnp.exp(scores - top), 0.0)
        return raised / jnp.sum(raised, axis=-1, keepdims=True)

    def head(i, second=False):
        start = i * HD + (HALF if second else 0)
        return slice(start, start + HD)

    def mine_head(i):
        return pl.ds(pl.multiple_of(g * HALF + i * HD, HD), HD)

    me8 = y * 2 + g
    for i in range(HEADS):
        probs = softmax(nt(qe[:, head(i)], skv[:, head(i)]), enc_mask)
        pe[i] = probs
        o = nn(probs.astype(BF), skv[:, head(i, True)])
        eb[me8, :, head(i)] = (neigh[:, mine_head(i)].astype(F32) + o).astype(BF)

    def ehalf(grp):
        return lambda r, k: eb.at[mod4(y + r) * 2 + grp, pl.ds(k * 128, 128), :]

    e_slot = comm.alloc(1)
    comm.send(e_slot, eb.at[me8], eb.at[me8], partner)
    ring_own, ring_other = Ring(comm, ehalf(g), yp, ym), Ring(comm, ehalf(1 - g), yp, ym)
    ring_own.start()
    next(run0)
    comm.recv(e_slot, eb.at[y * 2 + 1 - g], partner)
    ring_other.start()
    ring_own.forward()
    next(run0)
    ring_own.near()
    next(run0)
    ring_other.forward()
    ring_own.far()
    next(run0)
    ring_other.near()
    ring_other.far()
    next(run0)

    def esum(i, carry):
        v = eb[i].astype(F32)
        return carry + jnp.sum(v * v, axis=1, keepdims=True)

    inv_enc = lax.rsqrt(lax.fori_loop(0, 8, esum, jnp.zeros((ROWS, 1), F32)) / FEATURES + EPSILON)

    for h in range(2):

        def norm_enc(i, carry, h=h):
            gain = gb[i, 0, 1:2, h * HALF : (h + 1) * HALF]
            en[i * 2 + h] = (eb[i * 2 + h].astype(F32) * inv_enc * gain).astype(BF)
            return carry

        lax.fori_loop(0, 4, norm_enc, 0)

    for _ in range(3):
        next(run0)
    for rz in range(4):
        st0["wait"](rz)

    acc2[...] = jnp.zeros_like(acc2)

    def project_enc(i, carry):
        acc2[...] += nn(en[i], w0[pl.ds(pl.multiple_of(i * HALF, HALF), HALF), :])
        return carry

    lax.fori_loop(0, 8, project_enc, 0)
    nkv[...] = acc2[...].astype(BF)

    mx_slot = comm.alloc(1)
    rowdot = jnp.zeros((ROWS, 1), F32)
    for i in range(HEADS):
        q, k, v = dq[:, head(i)], nkv[:, head(i)], nkv[:, head(i, True)]
        ct = cot[:, mine_head(i)]
        probs = softmax(nt(q, k), dec_mask)
        rounded = probs.astype(BF)
        mxs[:, head(i)] = nn(rounded, v).astype(BF)
        grad_values = tn(rounded, ct)
        grad_probs = nt(ct, v)
        grad_scores = probs * (grad_probs - jnp.sum(grad_probs * probs, axis=-1, keepdims=True))
        grad_keys = tn(grad_scores.astype(BF), q) * SCALE
        rowdot = rowdot + jnp.sum(
            grad_keys * k.astype(F32) + grad_values * v.astype(F32), axis=1, keepdims=True
        )
        g2[:, head(i)] = grad_keys.astype(BF)
        g2[:, head(i, True)] = grad_values.astype(BF)
    mx_copy = comm.copy(mx_slot, mxs, mxr, partner)

    rd[y] = as_row(rowdot)
    rd_base = comm.alloc(4)
    small_start(rd, rd_base)

    def back_enc(r, h):
        b = mod4(y + r) * 2 + h
        rows = pl.ds(pl.multiple_of(b * HALF, HALF), HALF)
        pb[b] = nt(g2[...], w0[rows, :]).astype(BF)

    def scatter_of(h, j):
        return Scatter(
            comm,
            lambda r: pb.at[mod4(y + r) * 2 + h],
            (rba.at[j, 0], rba.at[j, 1], rbb.at[j, 0], rbb.at[j, 1]),
            yp, ym, ROWS,
        )

    away, home = scatter_of(1 - g, 0), scatter_of(g, 1)
    back_enc(2, 1 - g)
    away.first()
    back_enc(1, 1 - g)
    back_enc(-1, 1 - g)
    away.second()
    back_enc(2, g)
    home.first()
    back_enc(1, g)
    back_enc(-1, g)
    away.third()
    home.second()

    @pl.when(g == 1)
    def _():
        mx_copy.start()

    back_enc(0, 1 - g)
    back_enc(0, g)
    small_wait(rd, rd_base)
    rdp[0] = rd[0] + rd[1] + rd[2] + rd[3]
    comm.send(rd_base + 3, rdp.at[0], rdp.at[1], partner)
    ysum[...] = away.total().astype(BF)
    r3_slot = comm.alloc(1)
    comm.send(r3_slot, ysum, r3, partner)
    home.third()
    grad_in = home.total()
    comm.recv(rd_base + 3, rdp.at[1], partner)
    dot_all = as_col(rdp[0] + rdp[1])
    comm.recv(r3_slot, r3, partner)
    grad_in = grad_in + r3[...].astype(F32)
    grad_enc = (
        inv_enc * gb[y, 0, 1:2, mine] * grad_in
        - eb[me8].astype(F32) * (inv_enc * inv_enc * dot_all / FEATURES)
    ).astype(BF)

    rowdot1 = jnp.zeros((TOK, 1), F32)
    for i in range(HEADS):
        q, k, v = qe[:, head(i)], skv[:, head(i)], skv[:, head(i, True)]
        go = grad_enc[:, head(i)]
        probs = pe[i]
        grad_values = tn(probs.astype(BF), go)
        grad_probs = nt(go, v)
        grad_scores = probs * (grad_probs - jnp.sum(grad_probs * probs, axis=-1, keepdims=True))
        grad_keys = tn(grad_scores.astype(BF), q) * SCALE
        rowdot1 = rowdot1 + jnp.sum(
            grad_keys * k.astype(F32) + grad_values * v.astype(F32), axis=1, keepdims=True
        )
        g1[:, head(i)] = grad_keys.astype(BF)
        g1[:, head(i, True)] = grad_values.astype(BF)

    rd1[y] = as_row(rowdot1)
    rd1_base = comm.alloc(4)
    small_start(rd1, rd1_base)

    def back_state(r, h):
        b = mod4(y + r) * 2 + h
        rows = pl.ds(pl.multiple_of(b * HALF, HALF), HALF)
        pb1[b] = nt(g1[...], w1[rows, :]).astype(BF)

    def scatter_state(h):
        return Scatter(
            comm,
            lambda r: pb1.at[mod4(y + r) * 2 + h],
            (rca.at[h, 0], rca.at[h, 1], rcb.at[h, 0], rcb.at[h, 1]),
            yp, ym, TOK,
        )

    sc = [scatter_state(0), scatter_state(1)]
    for h in range(2):
        back_state(2, h)
        sc[h].first()
        back_state(1, h)
        back_state(-1, h)
        sc[h].second()
    sc[0].third()
    back_state(0, 0)
    back_state(0, 1)
    sc[1].third()
    small_wait(rd1, rd1_base)
    rdp1[0] = rd1[0] + rd1[1] + rd1[2] + rd1[3]
    comm.send(rd1_base + 3, rdp1.at[0], rdp1.at[1], partner)
    t3_slot = comm.alloc(2)
    t3_copies = [comm.copy(t3_slot + h, ysum1.at[h], t3.at[h], partner) for h in range(2)]
    for h in range(2):
        ysum1[h] = sc[h].total().astype(BF)

        @pl.when(g == 0)
        def _(h=h):
            t3_copies[h].start()

    comm.recv(rd1_base + 3, rdp1.at[1], partner)

    @pl.when(g == 0)
    def _():
        mx_copy.wait_recv()
        for h in range(2):
            theirs = mxr if h == 1 else mxs
            cols = slice(h * HALF, (h + 1) * HALF)
            out[:, cols] = states[:, cols].astype(F32) + theirs[...].astype(F32)
        for copy in t3_copies:
            copy.wait_send()

    @pl.when(g == 1)
    def _():
        dot_state = as_col(rdp1[0] + rdp1[1])
        factor = inv_state * inv_state * dot_state / FEATURES
        for h in range(2):
            t3_copies[h].wait_recv()
            cols = slice(h * HALF, (h + 1) * HALF)
            total = ysum1[h].astype(F32) + t3[h].astype(F32)
            out[:, cols] = (
                inv_state * gb[y, 1, 0:1, cols] * total - states[:, cols].astype(F32) * factor
            )
        mx_copy.wait_send()

    comm.drain()
    done1()
    done0()


def per_device(states, neighbours, cotangent, span_of, counts, kv_weight, gains):
    wsrc = kv_weight.reshape(TOK, 2, 2, HALF).transpose(2, 0, 1, 3).reshape(2, TOK, COLS)
    vmem, smem, hbm = (
        pl.BlockSpec(memory_space=m) for m in (pltpu.VMEM, pltpu.SMEM, pl.ANY)
    )

    def bf(*shape):
        return pltpu.VMEM(shape, BF)

    def f32(*shape):
        return pltpu.VMEM(shape, F32)

    scratch = [
        bf(FEATURES, COLS),
        bf(FEATURES, COLS),
        bf(4, TOK, COLS),
        bf(4, TOK, COLS),
        f32(4, 2, 8, COLS),
        f32(4, 8, ROWS),
        bf(8, ROWS, HALF),
        bf(8, ROWS, HALF),
        f32(TOK, COLS),
        bf(TOK, COLS),
        bf(ROWS, HALF),
        f32(HEADS, ROWS, TOK),
        f32(ROWS, COLS),
        bf(ROWS, COLS),
        bf(TOK, HALF),
        bf(ROWS, COLS),
        bf(8, ROWS, HALF),
        bf(2, 2, ROWS // 2, HALF),
        bf(2, 2, ROWS, HALF),
        bf(ROWS, HALF),
        bf(ROWS, HALF),
        bf(TOK, COLS),
        bf(8, TOK, HALF),
        bf(2, 2, TOK // 2, HALF),
        bf(2, 2, TOK, HALF),
        bf(2, TOK, HALF),
        bf(2, TOK, HALF),
        f32(4, 8, ROWS),
        f32(2, 8, ROWS),
        f32(4, 8, TOK),
        f32(2, 8, TOK),
        bf(TOK, HALF),
        bf(TOK, HALF),
        pltpu.SemaphoreType.DMA((SEMS,)),
        pltpu.SemaphoreType.DMA((SEMS,)),
        pltpu.SemaphoreType.DMA((2,)),
    ]
    result = pl.pallas_call(
        kernel,
        out_shape=jax.ShapeDtypeStruct((TOK, COLS), F32),
        in_specs=[hbm, vmem, vmem, vmem, smem, smem, vmem],
        out_specs=vmem,
        scratch_shapes=scratch,
        compiler_params=pltpu.CompilerParams(
            collective_id=0, has_side_effects=True, vmem_limit_bytes=60 * 1024 * 1024
        ),
        name="spanned_attention",
    )(
        wsrc,
        states,
        neighbours.reshape(ROWS, COLS),
        cotangent,
        span_of,
        counts,
        gains.reshape(2, COLS),
    )
    return result[None]


def solution(mesh):
    return jax.shard_map(
        per_device,
        mesh=mesh,
        in_specs=(
            P("dp", "mp"),
            P("dp", None, "mp"),
            P("dp", "mp"),
            P("dp"),
            P("dp"),
            P("group", "dp", None, "mp"),
            P("group", None, "mp"),
        ),
        out_specs=P("group", "dp", "mp"),
        check_vma=False,
    )
```

time: 406 us -> 160 us (0.39)
  waiting for transfers between devices: 252 us -> 0 us
  Pallas kernels: 0 us -> 153 us
  matrix products: 61.9 us -> 0 us
  blocking collectives: 38.7 us -> 0 us
  other arithmetic: 14.5 us -> 0 us
  between operations: 14.1 us -> 0.68 us
  local copies, waits for them, and re-layouts: 18.4 us -> 5.82 us
  starting transfers between devices: 5.35 us -> 0 us
    all_gather x3 -> x0, waiting for transfers between devices: 161 us -> none  [the longest x1 111 us: per_device(): whole_rows = lax.all_gather(kv_weight[0], 'dp', axis=0, tiled=True)]
    pallas_call x0 -> x1, Pallas kernels: none -> 153 us  [per_device(): pl.pallas_call(kernel, out_shape=jax.ShapeDtypeStruct((TOK, COLS), F32),...]
    dot_general x13 -> x0, matrix products: 59.2 us -> none  [the longest x2 24.4 us: project_back(): jnp.einsum('nkf,wkf->nw', grad_pair, weight_rows, preferred_element_type=...]
    reduce_scatter x2 -> x0, waiting for transfers between devices: 57.5 us -> none  [the longest x1 32.4 us: per_device(): lax.psum_scatter(neigh_partial.astype(jnp.bfloat16), 'mp', scatter_dimens...]
    psum x4 -> x0, blocking collectives: 38.7 us -> none  [the longest x1 10.9 us: per_device(): enc_total = lax.psum(jnp.sum(arrived_f * arrived_f, axis=1), 'mp')]
    ppermute x2 -> x0, waiting for transfers between devices: 32.7 us -> none  [passed_along(): return lax.ppermute(array, axis, pairs)]
    convert_element_type x4 -> x0, other arithmetic: 5.49 us -> none  [the longest x1 1.8 us: per_device(): (state_f * inv_state[:, None] * gain_first).astype(jnp.bfloat16)]
    ppermute x2 -> x0, starting transfers between devices: 5 us -> none  [passed_along(): return lax.ppermute(array, axis, pairs)]
  transfers between devices with their start and end apart: 7 -> 0, of which waited for: 7 -> 0; matrix products, arithmetic and copies ran while one was open for 2% -> 0% of each run, Pallas kernels for 0% -> 0%
where the time goes in v1:
time: 160 us; the launch traced here: 159 us
  Pallas kernels  153 us (96%)
  local copies, waits for them, and re-layouts  5.82 us (4%)
    pallas_call x1, Pallas kernels, per_device(): pl.pallas_call(kernel, out_shape=jax.ShapeDtypeStruct((TOK, COLS), F32),...  153 us
    reshape x3, local copies, waits for them, and re-layouts, per_device(): kv_weight.reshape(TOK, 2, 2, HALF).transpose(2, 0, 1, 3)  3.93 us

profile of v1, /device:TPU:2, one launch (start us, length us, event | category | flops | bytes accessed | tf_op | source)
XLA Modules:
  0.0 159.4 jit_solution(18145835804559982616)
XLA Ops:
  0.7 2.4 %reshape.12 = bf16[128,2,2,512]{3,2,1,0:T(2,128)(2,1)S(1)} reshape(bf16[1,128,2,1024]{3,2,1,0:T(2,128)(2,1)} %param.12) | data formatting | bytes 1048576 | tf_op jit(solution)/shard_map/reshape | solution.py:604
  3.0 0.4 copy.10
  3.4 1.2 reshape.13.wsrc
  4.6 152.9 %spanned_attention.1 = f32[128,1024]{1,0:T(8,128)} custom-call(bf16[2,128,1024]{2,1,0:T(8,128)(2,1)} %reshape.13.wsrc, bf16[128,1024]{1,0:T(8,128)(2,1)} %states.1, bf16[256,1024]{1,0:T(8,128)(2,1)} %bitcast.8, bf16[128,1024]{1,0:T(8,128)(2,1)} %cot.1, s32[4]{0:T(128)} %span.1, s32[1]{0:T(128)S(6)} %copy.12.counts, f32[2,1024]{1,0:T(2,128)} %bitcast.9), custom_call_target="tpu_custom_call" | custom-call | tf_op jit(solution)/shard_map/spanned_attention/pallas_call | solution.py:653
  157.5 1.9 %copy.13 = f32[1,128,1024]{2,1,0:T(8,128)} copy(f32[1,128,1024]{2,1,0:T(8,128)} %bitcast.7) | data formatting | bytes 1048576

commit v2 on v1

--- a/solution.py
+++ b/solution.py
@@ -144,8 +144,8 @@
 
 
 def kernel(
-    wsrc, states, neigh, cot, span, counts, gains, out,
-    w1, w0, sx, xn, gb, ns, eb, en, acc1, skv, qe, pe, acc2, nkv, dq, g2, pb, rba, rbb, r3, ysum,
+    keys, values, states_in, neigh_in, cot_in, span, counts, gains, out,
+    w, theirs, states, neigh, cot, sx, xn, gb, ns, eb, en, acc1, skv, qe, pe, acc2, nkv, dq, g2, pb, rba, rbb, r3, ysum,
     g1, pb1, rca, rcb, t3, ysum1, rd, rdp, rd1, rdp1, mxs, mxr,
     ssem, rsem, lsem,
 ):
@@ -171,8 +171,26 @@
     sibling = {"dp": d + 1 - 2 * c}
     xp, xm, zp, zm, yp, ym, y2 = at_x(1), at_x(-1), at_z(1), at_z(-1), at_y(1), at_y(-1), at_y(2)
 
+    across = {"group": 1 - g, "dp": x * 8 + mod4(zh + 2 * g - 1) * 2 + c}
+    fetch = [
+        pltpu.make_async_copy(src, dst, lsem.at[i])
+        for i, (src, dst) in enumerate(((states_in, states), (neigh_in, neigh), (cot_in, cot)))
+    ]
+    own_start = pl.multiple_of(d * TOK, TOK)
+    local = []
+    for i, (src, grp, dst) in enumerate(
+        (src, grp, dst)
+        for grp, dst in ((g, w.at[g, pl.ds(own_start, TOK), :]), (1 - g, theirs))
+        for src in (keys, values)
+    ):
+        cols = pl.ds(pl.multiple_of(grp * HALF, HALF), HALF)
+        to = dst.at[:, pl.ds((i % 2) * HALF, HALF)]
+        local.append(pltpu.make_async_copy(src.at[:, cols], to, lsem.at[3 + i]))
+        local[-1].start()
+    for copy in fetch:
+        copy.start()
     barrier = pltpu.get_barrier_semaphore()
-    peers = (partner, sibling, xp, xm, zp, zm, yp, ym, y2)
+    peers = (partner, sibling, xp, xm, zp, zm, yp, ym, y2, across)
     for dev in peers:
         pl.semaphore_signal(barrier, inc=1, device_id=dev, device_id_type=pl.DeviceIdType.MESH)
     pl.semaphore_wait(barrier, len(peers))
@@ -181,107 +199,123 @@
         return pl.multiple_of((mod4(x + rx) * 8 + mod4(zh + rz) * 2 + core) * TOK, TOK)
 
     own_rows = pl.ds(wrow(0, 0, c), TOK)
-
-    def exchange(w, owner):
-        local = pltpu.make_async_copy(wsrc.at[g], w.at[own_rows, :], lsem.at[owner])
-        away = comm.copy(comm.alloc(1), wsrc.at[1 - g], w.at[own_rows, :], partner)
-
-        @pl.when(g == owner)
-        def _():
-            away.start()
-            local.start()
-
-        def ready():
-            @pl.when(g == owner)
-            def _():
-                local.wait()
-
-            @pl.when(g != owner)
-            def _():
-                away.wait_recv()
-
-        def done():
-            @pl.when(g == owner)
-            def _():
-                away.wait_send()
-
-        return ready, done
-
-    ready1, done1 = exchange(w1, 1)
-    ready0, done0 = exchange(w0, 0)
-
-    def gather(w, ready, state):
-        def block(rx, rz, core):
-            return w.at[pl.ds(wrow(rx, rz, core), TOK), :]
-
-        def half(rx, rz, k):
-            return w.at[pl.ds(pl.multiple_of(wrow(rx, rz, c) + k * 64, 64), 64), :]
-
-        sib_base = comm.alloc(16)
-
-        def sib(rx, rz):
-            comm.send(sib_base + (rx % 4) * 4 + rz % 4, block(rx, rz, c), block(rx, rz, c), sibling)
-
-        def sib_wait(rz):
-            for rx in range(4):
-                comm.recv(sib_base + rx * 4 + rz % 4, block(rx, rz, 1 - c), sibling)
-
-        state["wait"] = sib_wait
-        zr = Ring(comm, lambda r, k: half(0, r, k), zp, zm)
-        xr = {
-            rz: Ring(comm, functools.partial(lambda rz, r, k: half(r, rz, k), rz), xp, xm)
-            for rz in (0, -1, 1, 2)
-        }
-        ready()
-        zr.start()
-        yield
-        xr[0].start()
-        sib(0, 0)
-        yield
-        zr.forward()
-        xr[0].forward()
-        yield
-        zr.near()
-        for rz in (-1, 1):
-            xr[rz].start()
-            sib(0, rz)
-        yield
-        xr[0].near()
-        sib(-1, 0)
-        sib(1, 0)
-        xr[0].far()
-        sib(2, 0)
-        yield
-        zr.far()
-        xr[2].start()
-        sib(0, 2)
-        yield
-        xr[-1].forward()
-        xr[1].forward()
-        yield
-        for rz in (-1, 1):
-            xr[rz].near()
-            sib(-1, rz)
-            sib(1, rz)
-        xr[2].forward()
-        yield
-        for rz in (-1, 1):
-            xr[rz].far()
-            sib(2, rz)
-        yield
-        xr[2].near()
-        sib(-1, 2)
-        sib(1, 2)
-        xr[2].far()
-        sib(2, 2)
-        yield
-
-    st1, st0 = {}, {}
-    run1, run0 = gather(w1, ready1, st1), gather(w0, ready0, st0)
+    ORDER = {1: (0, -1, 1, 2), 0: (0, 1, -1, 2)}
+    PLAN = {
+        1: [(1, 0), (1, 1), (1, 2), (1, 3), (0, 0), (0, 1), (0, 2), (0, 3)],
+        0: [(0, 0), (1, 0), (1, 1), (1, 2), (1, 3), (0, 1), (0, 2), (0, 3)],
+    }
+    zbase = {m: comm.alloc(10) for m in (0, 1)}
+    zsent = {0: [], 1: []}
+
+    def either(fn):
+        for grp in (0, 1):
+            pl.when(g == grp)(functools.partial(fn, grp))
+
+    def zblock(m, rz):
+        return w.at[m, pl.ds(wrow(0, rz, c), TOK), :]
+
+    def zhalf(m, rz, k):
+        return w.at[m, pl.ds(pl.multiple_of(wrow(0, rz, c) + k * 64, 64), 64), :]
+
+    def zsend(grp, slot, ref, dev, src=None):
+        def make():
+            dst = ref()
+            return comm.copy(slot, dst if src is None else src(), dst, dev)
+
+        make().start()
+        zsent[grp].append(make)
+
+    def zout(grp):
+        m, base = grp, zbase[grp]
+        for slot, dev in ((6, partner), (7, across)):
+            zsend(grp, base + slot, lambda: zblock(m, 0), dev, lambda: theirs)
+        for slot, k, dev in ((0, 0, zp), (2, 1, zm), (1, 1, zp), (3, 0, zm)):
+            zsend(grp, base + slot, lambda k=k: zhalf(m, 0, k), dev)
+
+    def zarrive(grp, m, i):
+        base, rz = zbase[m], ORDER[m][i]
+        if grp == m:
+            if i == 0:
+                return
+            if i == 1:
+                comm.recv(base, zhalf(m, -1, 0), zm)
+                zsend(grp, base + 4, lambda: zhalf(m, -1, 0), zp)
+                comm.recv(base + 2, zhalf(m, 1, 1), zp)
+                zsend(grp, base + 5, lambda: zhalf(m, 1, 1), zm)
+            if rz == -1:
+                comm.recv(base + 1, zhalf(m, -1, 1), zm)
+            elif rz == 1:
+                comm.recv(base + 3, zhalf(m, 1, 0), zp)
+            else:
+                comm.recv(base + 4, zhalf(m, 2, 0), zm)
+                comm.recv(base + 5, zhalf(m, 2, 1), zp)
+            return
+        if i == 0:
+            comm.recv(base + 6, zblock(m, 0), partner)
+            zsend(grp, base + 8, lambda: zblock(m, 0), zm if m == 1 else zp)
+        elif i == 1:
+            comm.recv(base + 7, zblock(m, rz), across)
+            zsend(grp, base + 9, lambda: zblock(m, rz), zp if m == 1 else zm)
+        else:
+            comm.recv(base + 6 + i, zblock(m, rz), zp)
+
+    def plan(grp, s):
+        m, i = PLAN[grp][s]
+        return m, ORDER[m][i]
+
+    class Slot:
+        def __init__(self, s):
+            (m0, r0), (m1, r1) = plan(0, s), plan(1, s)
+            self.s, self.m, self.rz = s, m0 + (m1 - m0) * g, r0 + (r1 - r0) * g
+            self.ring = Ring(comm, self.half, xp, xm)
+            self.sib = comm.alloc(4)
+
+        def half(self, r, k):
+            return w.at[self.m, pl.ds(pl.multiple_of(wrow(r, self.rz, c) + k * 64, 64), 64), :]
+
+        def share(self, *rels):
+            for rx in rels:
+                block = w.at[self.m, pl.ds(wrow(rx, self.rz, c), TOK), :]
+                comm.send(self.sib + rx % 4, block, block, sibling)
+
+        def start(self):
+            either(lambda grp: zarrive(grp, *PLAN[grp][self.s]))
+            self.ring.start()
+            self.share(0)
+
+        def forward(self):
+            self.ring.forward()
+
+        def rest(self):
+            self.ring.near()
+            self.share(-1, 1)
+            self.ring.far()
+            self.share(2)
+
+    slots = [Slot(s) for s in range(8)]
+    sib_first = slots[0].sib
+    sib_step = slots[1].sib - slots[0].sib
+
+    def shared(m, i):
+        s0, s1 = (PLAN[grp].index((m, i)) for grp in (0, 1))
+        rz = ORDER[m][i]
+        for rx in range(4):
+            comm.recv(
+                sib_first + (s0 + (s1 - s0) * g) * sib_step + rx,
+                w.at[m, pl.ds(wrow(rx, rz, 1 - c), TOK), :],
+                sibling,
+            )
+
+    for copy in local:
+        copy.wait()
+    pl.when(g == 1)(lambda: zout(1))
+    slots[0].start()
 
     def shalf(r, k):
         return sx.at[mod4(y + r), pl.ds(k * 64, 64), :]
 
+    for copy in fetch:
+        copy.wait()
     sx[y] = states[...]
     even = lax.broadcasted_iota(jnp.int32, (8, COLS), 0) % 2 == 0
     gb[y, g] = jnp.where(even, gains[0:1, :], gains[1:2, :])
@@ -289,8 +323,6 @@
     sring.start()
     gain_slot = comm.alloc(4)
     comm.send(gain_slot, gb.at[y, g], gb.at[y, g], partner)
-    next(run1)
-    next(run1)
 
     def small_start(buf, base):
         for i, (r, dev) in enumerate(((1, yp), (-1, ym), (2, y2))):
@@ -306,8 +338,10 @@
     small_start(ns, ns_base)
     comm.recv(gain_slot, gb.at[y, 1 - g], partner)
     small_start(gb, gain_slot + 1)
+    slots[0].forward()
     sring.forward()
-    next(run1)
+    slots[1].start()
+    slots[0].rest()
     sring.near()
     sring.far()
     small_wait(ns, ns_base)
@@ -329,33 +363,38 @@
     inv_neigh = as_col(lax.rsqrt((ns[0] + ns[1] + ns[2] + ns[3]) / FEATURES + EPSILON))
     qe[...] = (neigh[:, mine].astype(F32) * inv_neigh * gb[y, 1, 1:2, mine]).astype(BF)
 
-    def project_states(rz, first):
-        st1["wait"](rz)
-        z = mod4(zh + rz)
-
-        def step(i, carry):
-            rows = pl.ds(pl.multiple_of((i * 4 + z) * 256, 256), 256)
-            part = nn(xn[i, :, pl.ds(pl.multiple_of(z * 256, 256), 256)], w1[rows, :])
+    def chunk_rows(i, z):
+        return pl.ds(pl.multiple_of((i * 4 + z) * 256, 256), 256)
+
+    def project_states(i):
+        shared(1, i)
+        z = mod4(zh + ORDER[1][i])
+
+        def step(k, carry):
+            part = nn(xn[k, :, pl.ds(pl.multiple_of(z * 256, 256), 256)], w[1, chunk_rows(k, z), :])
             acc1[...] += part
             return carry
 
-        if first:
-            acc1[...] = jnp.zeros_like(acc1)
         lax.fori_loop(0, 4, step, 0)
 
-    next(run1)
-    next(run1)
-    next(run1)
-    next(run0)
-    project_states(0, True)
-    next(run1)
-    next(run1)
-    next(run1)
-    next(run0)
-    project_states(-1, False)
-    project_states(1, False)
-    next(run1)
-    project_states(2, False)
+    acc1[...] = jnp.zeros_like(acc1)
+    slots[1].forward()
+    slots[2].start()
+    slots[1].rest()
+    pl.when(g == 0)(lambda: zout(0))
+    project_states(0)
+    slots[2].forward()
+    slots[3].start()
+    slots[2].rest()
+    project_states(1)
+    slots[3].forward()
+    slots[4].start()
+    slots[3].rest()
+    project_states(2)
+    slots[4].forward()
+    slots[5].start()
+    slots[4].rest()
+    project_states(3)
     skv[...] = acc1[...].astype(BF)
 
     base_span = d * 2
@@ -400,19 +439,21 @@
     comm.send(e_slot, eb.at[me8], eb.at[me8], partner)
     ring_own, ring_other = Ring(comm, ehalf(g), yp, ym), Ring(comm, ehalf(1 - g), yp, ym)
     ring_own.start()
-    next(run0)
+    slots[5].forward()
+    slots[6].start()
     comm.recv(e_slot, eb.at[y * 2 + 1 - g], partner)
     ring_other.start()
     ring_own.forward()
-    next(run0)
+    slots[5].rest()
     ring_own.near()
-    next(run0)
+    slots[6].forward()
+    slots[7].start()
     ring_other.forward()
     ring_own.far()
-    next(run0)
+    slots[6].rest()
     ring_other.near()
     ring_other.far()
-    next(run0)
+    slots[7].forward()
 
     def esum(i, carry):
         v = eb[i].astype(F32)
@@ -429,18 +470,23 @@
 
         lax.fori_loop(0, 4, norm_enc, 0)
 
-    for _ in range(3):
-        next(run0)
-    for rz in range(4):
-        st0["wait"](rz)
-
     acc2[...] = jnp.zeros_like(acc2)
 
-    def project_enc(i, carry):
-        acc2[...] += nn(en[i], w0[pl.ds(pl.multiple_of(i * HALF, HALF), HALF), :])
-        return carry
-
-    lax.fori_loop(0, 8, project_enc, 0)
+    def project_enc(i):
+        shared(0, i)
+        z = mod4(zh + ORDER[0][i])
+
+        def step(k, carry):
+            cols = pl.ds(pl.multiple_of((z % 2) * 256, 256), 256)
+            acc2[...] += nn(en[k * 2 + z // 2, :, cols], w[0, chunk_rows(k, z), :])
+            return carry
+
+        lax.fori_loop(0, 4, step, 0)
+
+    for i in range(3):
+        project_enc(i)
+    slots[7].rest()
+    project_enc(3)
     nkv[...] = acc2[...].astype(BF)
 
     mx_slot = comm.alloc(1)
@@ -469,7 +515,7 @@
     def back_enc(r, h):
         b = mod4(y + r) * 2 + h
         rows = pl.ds(pl.multiple_of(b * HALF, HALF), HALF)
-        pb[b] = nt(g2[...], w0[rows, :]).astype(BF)
+        pb[b] = nt(g2[...], w[0, rows, :]).astype(BF)
 
     def scatter_of(h, j):
         return Scatter(
@@ -537,7 +583,7 @@
     def back_state(r, h):
         b = mod4(y + r) * 2 + h
         rows = pl.ds(pl.multiple_of(b * HALF, HALF), HALF)
-        pb1[b] = nt(g1[...], w1[rows, :]).astype(BF)
+        pb1[b] = nt(g1[...], w[1, rows, :]).astype(BF)
 
     def scatter_state(h):
         return Scatter(
@@ -576,9 +622,9 @@
     def _():
         mx_copy.wait_recv()
         for h in range(2):
-            theirs = mxr if h == 1 else mxs
+            heads_out = mxr if h == 1 else mxs
             cols = slice(h * HALF, (h + 1) * HALF)
-            out[:, cols] = states[:, cols].astype(F32) + theirs[...].astype(F32)
+            out[:, cols] = states[:, cols].astype(F32) + heads_out[...].astype(F32)
         for copy in t3_copies:
             copy.wait_send()
 
@@ -596,12 +642,11 @@
         mx_copy.wait_send()
 
     comm.drain()
-    done1()
-    done0()
+    either(lambda grp: [make().wait_send() for make in zsent[grp]] and None)
 
 
 def per_device(states, neighbours, cotangent, span_of, counts, kv_weight, gains):
-    wsrc = kv_weight.reshape(TOK, 2, 2, HALF).transpose(2, 0, 1, 3).reshape(2, TOK, COLS)
+    keys, values = kv_weight[0, :, 0, :], kv_weight[0, :, 1, :]
     vmem, smem, hbm = (
         pl.BlockSpec(memory_space=m) for m in (pltpu.VMEM, pltpu.SMEM, pl.ANY)
     )
@@ -613,8 +658,11 @@
         return pltpu.VMEM(shape, F32)
 
     scratch = [
-        bf(FEATURES, COLS),
-        bf(FEATURES, COLS),
+        bf(2, FEATURES, COLS),
+        bf(TOK, COLS),
+        bf(TOK, COLS),
+        bf(ROWS, COLS),
+        bf(TOK, COLS),
         bf(4, TOK, COLS),
         bf(4, TOK, COLS),
         f32(4, 2, 8, COLS),
@@ -648,12 +696,12 @@
         bf(TOK, HALF),
         pltpu.SemaphoreType.DMA((SEMS,)),
         pltpu.SemaphoreType.DMA((SEMS,)),
-        pltpu.SemaphoreType.DMA((2,)),
+        pltpu.SemaphoreType.DMA((7,)),
     ]
     result = pl.pallas_call(
         kernel,
         out_shape=jax.ShapeDtypeStruct((TOK, COLS), F32),
-        in_specs=[hbm, vmem, vmem, vmem, smem, smem, vmem],
+        in_specs=[hbm, hbm, hbm, hbm, hbm, smem, smem, vmem],
         out_specs=vmem,
         scratch_shapes=scratch,
         compiler_params=pltpu.CompilerParams(
@@ -661,7 +709,8 @@
         ),
         name="spanned_attention",
     )(
-        wsrc,
+        keys,
+        values,
         states,
         neighbours.reshape(ROWS, COLS),
         cotangent,

time: 160 us -> 146 us (0.912)
  Pallas kernels: 153 us -> 140 us
    pallas_call x1, Pallas kernels: 153 us -> 140 us  [per_device(): pl.pallas_call(kernel, out_shape=jax.ShapeDtypeStruct((TOK, COLS), F32),...]
    reshape x3 -> x0, local copies, waits for them, and re-layouts: 3.93 us -> none  [per_device(): kv_weight.reshape(TOK, 2, 2, HALF).transpose(2, 0, 1, 3)]
    slice x0 -> x1, local copies, waits for them, and re-layouts: none -> 2.1 us  [per_device(): keys, values = (kv_weight[0, :, 0, :], kv_weight[0, :, 1, :])]
where the time goes in v2:
time: 146 us
  Pallas kernels  140 us (96%)
  local copies, waits for them, and re-layouts  4.93 us (3%)
    pallas_call x1, Pallas kernels, per_device(): pl.pallas_call(kernel, out_shape=jax.ShapeDtypeStruct((TOK, COLS), F32),...  140 us

profile of v2, /device:TPU:2, one launch (start us, length us, event | category | flops | bytes accessed | tf_op | source)
XLA Modules:
  0.0 145.5 jit_solution(9808132309565041513)
XLA Ops:
  0.0 2.1 %fusion = (bf16[1,128,1,1024]{3,2,1,0:T(2,128)(2,1)S(1)}, bf16[1,128,1,1024]{3,2,1,0:T(2,128)(2,1)S(1)}) fusion(bf16[1,128,2,1024]{3,2,1,0:T(2,128)(2,1)} %param.12), kind=kLoop, calls=%fused_computation.2 | loop fusion | bytes 1048576 | tf_op jit(solution)/shard_map/slice | solution.py:649
  2.1 0.9 copy_bitcast_fusion
  3.7 139.9 %spanned_attention.1 = f32[128,1024]{1,0:T(8,128)} custom-call(bf16[128,1024]{1,0:T(8,128)(2,1)} %get-tuple-element.8.keys, bf16[128,1024]{1,0:T(8,128)(2,1)} %get-tuple-element.7.values, bf16[128,1024]{1,0:T(8,128)(2,1)} %states_in.1, bf16[256,1024]{1,0:T(8,128)(2,1)} %bitcast.8, bf16[128,1024]{1,0:T(8,128)(2,1)} %cot_in.1, s32[4]{0:T(128)} %span.1, ...), custom_call_target="tpu_custom_call" | custom-call | tf_op jit(solution)/shard_map/spanned_attention/pallas_call | solution.py:701
  143.6 1.9 %copy.16 = f32[1,128,1024]{2,1,0:T(8,128)} copy(f32[1,128,1024]{2,1,0:T(8,128)} %bitcast.7) | data formatting | bytes 1048576

commit v3 on v2

--- a/solution.py
+++ b/solution.py
@@ -20,7 +20,9 @@
 SCALE = HD ** (-0.5)
 BF = jnp.bfloat16
 F32 = jnp.float32
-SEMS = 224
+SEMS = 320
+AROWS = TOK
+SPLIT = 64
 
 
 def nt(a, b):
@@ -144,8 +146,8 @@
 
 
 def kernel(
-    keys, values, states_in, neigh_in, cot_in, span, counts, gains, out,
-    w, theirs, states, neigh, cot, sx, xn, gb, ns, eb, en, acc1, skv, qe, pe, acc2, nkv, dq, g2, pb, rba, rbb, r3, ysum,
+    wide, states_in, neigh_in, cot_in, span, counts, gains, out,
+    w, theirs, states, neigh, cot, sx, xn, gb, ns, eb, en, acc1, skv, qe, pe, acc2, nkv, dq, g2, pb, lz, rba, rbb, r3, ysum,
     g1, pb1, rca, rcb, t3, ysum1, rd, rdp, rd1, rdp1, mxs, mxr,
     ssem, rsem, lsem,
 ):
@@ -176,46 +178,54 @@
         pltpu.make_async_copy(src, dst, lsem.at[i])
         for i, (src, dst) in enumerate(((states_in, states), (neigh_in, neigh), (cot_in, cot)))
     ]
-    own_start = pl.multiple_of(d * TOK, TOK)
     local = []
-    for i, (src, grp, dst) in enumerate(
-        (src, grp, dst)
-        for grp, dst in ((g, w.at[g, pl.ds(own_start, TOK), :]), (1 - g, theirs))
-        for src in (keys, values)
-    ):
-        cols = pl.ds(pl.multiple_of(grp * HALF, HALF), HALF)
-        to = dst.at[:, pl.ds((i % 2) * HALF, HALF)]
-        local.append(pltpu.make_async_copy(src.at[:, cols], to, lsem.at[3 + i]))
-        local[-1].start()
+    for i, (grp, dst) in enumerate(((g, w.at[g, x, zh, c]), (1 - g, theirs))):
+        for pair in range(2):
+            cols = pl.ds(pl.multiple_of(pair * COLS + grp * HALF, HALF), HALF)
+            to = dst.at[:, pl.ds(pair * HALF, HALF)]
+            local.append(pltpu.make_async_copy(wide.at[:, cols], to, lsem.at[3 + 2 * i + pair]))
+            local[-1].start()
     for copy in fetch:
         copy.start()
     barrier = pltpu.get_barrier_semaphore()
     peers = (partner, sibling, xp, xm, zp, zm, yp, ym, y2, across)
     for dev in peers:
         pl.semaphore_signal(barrier, inc=1, device_id=dev, device_id_type=pl.DeviceIdType.MESH)
+    for copy in fetch:
+        copy.wait()
+    nf = neigh[...].astype(F32)
+    sq_rows = as_row(jnp.sum(nf * nf, axis=1, keepdims=True))
+    sx[y] = states[...]
+    even = lax.broadcasted_iota(jnp.int32, (8, COLS), 0) % 2 == 0
+    gb[y, g] = jnp.where(even, gains[0:1, :], gains[1:2, :])
+    for copy in local:
+        copy.wait()
     pl.semaphore_wait(barrier, len(peers))
 
-    def wrow(rx, rz, core):
-        return pl.multiple_of((mod4(x + rx) * 8 + mod4(zh + rz) * 2 + core) * TOK, TOK)
-
-    own_rows = pl.ds(wrow(0, 0, c), TOK)
     ORDER = {1: (0, -1, 1, 2), 0: (0, 1, -1, 2)}
     PLAN = {
-        1: [(1, 0), (1, 1), (1, 2), (1, 3), (0, 0), (0, 1), (0, 2), (0, 3)],
+        1: [(1, 0), (0, 0), (1, 1), (1, 2), (1, 3), (0, 1), (0, 2), (0, 3)],
         0: [(0, 0), (1, 0), (1, 1), (1, 2), (1, 3), (0, 1), (0, 2), (0, 3)],
     }
     zbase = {m: comm.alloc(10) for m in (0, 1)}
     zsent = {0: [], 1: []}
 
+    def whole(m, rx, rz, core):
+        return w.at[m, mod4(x + rx), mod4(zh + rz), core]
+
+    def main(m, rx, rz, core):
+        return whole(m, rx, rz, core).at[pl.ds(0, AROWS), :]
+
+    def main_half(m, rx, rz, k):
+        rows = pl.ds(0, SPLIT) if k == 0 else pl.ds(SPLIT, AROWS - SPLIT)
+        return whole(m, rx, rz, c).at[rows, :]
+
     def either(fn):
         for grp in (0, 1):
             pl.when(g == grp)(functools.partial(fn, grp))
 
-    def zblock(m, rz):
-        return w.at[m, pl.ds(wrow(0, rz, c), TOK), :]
-
     def zhalf(m, rz, k):
-        return w.at[m, pl.ds(pl.multiple_of(wrow(0, rz, c) + k * 64, 64), 64), :]
+        return main_half(m, 0, rz, k)
 
     def zsend(grp, slot, ref, dev, src=None):
         def make():
@@ -225,10 +235,14 @@
         make().start()
         zsent[grp].append(make)
 
+    def zpartner(grp):
+        zsend(grp, zbase[grp] + 6, lambda: whole(grp, 0, 0, c), partner, lambda: theirs)
+
     def zout(grp):
         m, base = grp, zbase[grp]
-        for slot, dev in ((6, partner), (7, across)):
-            zsend(grp, base + slot, lambda: zblock(m, 0), dev, lambda: theirs)
+        zsend(
+            grp, base + 7, lambda: main(m, 0, 0, c), across, lambda: theirs.at[pl.ds(0, AROWS), :]
+        )
         for slot, k, dev in ((0, 0, zp), (2, 1, zm), (1, 1, zp), (3, 0, zm)):
             zsend(grp, base + slot, lambda k=k: zhalf(m, 0, k), dev)
 
@@ -251,13 +265,16 @@
                 comm.recv(base + 5, zhalf(m, 2, 1), zp)
             return
         if i == 0:
-            comm.recv(base + 6, zblock(m, 0), partner)
-            zsend(grp, base + 8, lambda: zblock(m, 0), zm if m == 1 else zp)
+            comm.recv(base + 6, whole(m, 0, 0, c), partner)
+            if m == 1:
+                zsend(grp, base + 8, lambda: main(m, 0, 0, c), zm)
         elif i == 1:
-            comm.recv(base + 7, zblock(m, rz), across)
-            zsend(grp, base + 9, lambda: zblock(m, rz), zp if m == 1 else zm)
+            if m == 0:
+                zsend(grp, base + 8, lambda: main(m, 0, 0, c), zp)
+            comm.recv(base + 7, main(m, 0, rz, c), across)
+            zsend(grp, base + 9, lambda: main(m, 0, rz, c), zp if m == 1 else zm)
         else:
-            comm.recv(base + 6 + i, zblock(m, rz), zp)
+            comm.recv(base + 6 + i, main(m, 0, rz, c), zp)
 
     def plan(grp, s):
         m, i = PLAN[grp][s]
@@ -271,11 +288,11 @@
             self.sib = comm.alloc(4)
 
         def half(self, r, k):
-            return w.at[self.m, pl.ds(pl.multiple_of(wrow(r, self.rz, c) + k * 64, 64), 64), :]
+            return main_half(self.m, r, self.rz, k)
 
         def share(self, *rels):
             for rx in rels:
-                block = w.at[self.m, pl.ds(wrow(rx, self.rz, c), TOK), :]
+                block = main(self.m, rx, self.rz, c)
                 comm.send(self.sib + rx % 4, block, block, sibling)
 
         def start(self):
@@ -298,27 +315,19 @@
 
     def shared(m, i):
         s0, s1 = (PLAN[grp].index((m, i)) for grp in (0, 1))
-        rz = ORDER[m][i]
         for rx in range(4):
             comm.recv(
                 sib_first + (s0 + (s1 - s0) * g) * sib_step + rx,
-                w.at[m, pl.ds(wrow(rx, rz, 1 - c), TOK), :],
+                main(m, rx, ORDER[m][i], 1 - c),
                 sibling,
             )
 
-    for copy in local:
-        copy.wait()
-    pl.when(g == 1)(lambda: zout(1))
+    either(zpartner)
     slots[0].start()
 
     def shalf(r, k):
         return sx.at[mod4(y + r), pl.ds(k * 64, 64), :]
 
-    for copy in fetch:
-        copy.wait()
-    sx[y] = states[...]
-    even = lax.broadcasted_iota(jnp.int32, (8, COLS), 0) % 2 == 0
-    gb[y, g] = jnp.where(even, gains[0:1, :], gains[1:2, :])
     sring = Ring(comm, shalf, yp, ym)
     sring.start()
     gain_slot = comm.alloc(4)
@@ -332,20 +341,22 @@
         for i, (r, dev) in enumerate(((-1, ym), (1, yp), (2, y2))):
             comm.recv(base + i, buf.at[mod4(y + r)], dev)
 
-    nf = neigh[...].astype(F32)
-    ns[y] = as_row(jnp.sum(nf * nf, axis=1, keepdims=True))
+    slots[0].forward()
+    pl.when(g == 1)(lambda: zout(1))
+    sring.forward()
+    ns[y] = sq_rows
     ns_base = comm.alloc(3)
     small_start(ns, ns_base)
     comm.recv(gain_slot, gb.at[y, 1 - g], partner)
     small_start(gb, gain_slot + 1)
-    slots[0].forward()
-    sring.forward()
     slots[1].start()
     slots[0].rest()
     sring.near()
     sring.far()
     small_wait(ns, ns_base)
     small_wait(gb, gain_slot + 1)
+    slots[1].forward()
+    slots[2].start()
 
     mine = pl.ds(pl.multiple_of(g * HALF, HALF), HALF)
     sums = jnp.zeros((TOK, 1), F32)
@@ -363,36 +374,31 @@
     inv_neigh = as_col(lax.rsqrt((ns[0] + ns[1] + ns[2] + ns[3]) / FEATURES + EPSILON))
     qe[...] = (neigh[:, mine].astype(F32) * inv_neigh * gb[y, 1, 1:2, mine]).astype(BF)
 
-    def chunk_rows(i, z):
-        return pl.ds(pl.multiple_of((i * 4 + z) * 256, 256), 256)
-
     def project_states(i):
         shared(1, i)
         z = mod4(zh + ORDER[1][i])
 
         def step(k, carry):
-            part = nn(xn[k, :, pl.ds(pl.multiple_of(z * 256, 256), 256)], w[1, chunk_rows(k, z), :])
+            part = nn(xn[k, :, pl.ds(pl.multiple_of(z * 256, 256), 256)], w[1, k, z].reshape(256, COLS))
             acc1[...] += part
             return carry
 
         lax.fori_loop(0, 4, step, 0)
 
     acc1[...] = jnp.zeros_like(acc1)
-    slots[1].forward()
-    slots[2].start()
     slots[1].rest()
-    pl.when(g == 0)(lambda: zout(0))
-    project_states(0)
     slots[2].forward()
     slots[3].start()
+    pl.when(g == 0)(lambda: zout(0))
     slots[2].rest()
-    project_states(1)
     slots[3].forward()
     slots[4].start()
     slots[3].rest()
-    project_states(2)
     slots[4].forward()
     slots[5].start()
+    project_states(0)
+    project_states(1)
+    project_states(2)
     slots[4].rest()
     project_states(3)
     skv[...] = acc1[...].astype(BF)
@@ -432,12 +438,19 @@
         o = nn(probs.astype(BF), skv[:, head(i, True)])
         eb[me8, :, head(i)] = (neigh[:, mine_head(i)].astype(F32) + o).astype(BF)
 
-    def ehalf(grp):
-        return lambda r, k: eb.at[mod4(y + r) * 2 + grp, pl.ds(k * 128, 128), :]
-
-    e_slot = comm.alloc(1)
+    def ehalf(grp, rows):
+        return lambda r, k: eb.at[mod4(y + r) * 2 + grp, pl.ds(k * rows, rows), :]
+
+    def elow(r, grp):
+        return eb.at[mod4(y + r) * 2 + grp, pl.ds(128, 128), :]
+
+    e_slot = comm.alloc(4)
+
+    def relay(i, r):
+        comm.send(e_slot + i, elow(r, g), elow(r, g), partner)
+
     comm.send(e_slot, eb.at[me8], eb.at[me8], partner)
-    ring_own, ring_other = Ring(comm, ehalf(g), yp, ym), Ring(comm, ehalf(1 - g), yp, ym)
+    ring_own, ring_other = Ring(comm, ehalf(g, 128), yp, ym), Ring(comm, ehalf(1 - g, 64), yp, ym)
     ring_own.start()
     slots[5].forward()
     slots[6].start()
@@ -446,14 +459,19 @@
     ring_own.forward()
     slots[5].rest()
     ring_own.near()
+    relay(1, 1)
+    relay(2, -1)
     slots[6].forward()
     slots[7].start()
     ring_other.forward()
     ring_own.far()
+    relay(3, 2)
     slots[6].rest()
     ring_other.near()
     ring_other.far()
     slots[7].forward()
+    for i, r in ((1, 1), (2, -1), (3, 2)):
+        comm.recv(e_slot + i, elow(r, 1 - g), partner)
 
     def esum(i, carry):
         v = eb[i].astype(F32)
@@ -478,7 +496,7 @@
 
         def step(k, carry):
             cols = pl.ds(pl.multiple_of((z % 2) * 256, 256), 256)
-            acc2[...] += nn(en[k * 2 + z // 2, :, cols], w[0, chunk_rows(k, z), :])
+            acc2[...] += nn(en[k * 2 + z // 2, :, cols], w[0, k, z].reshape(256, COLS))
             return carry
 
         lax.fori_loop(0, 4, step, 0)
@@ -491,21 +509,29 @@
 
     mx_slot = comm.alloc(1)
     rowdot = jnp.zeros((ROWS, 1), F32)
-    for i in range(HEADS):
-        q, k, v = dq[:, head(i)], nkv[:, head(i)], nkv[:, head(i, True)]
-        ct = cot[:, mine_head(i)]
-        probs = softmax(nt(q, k), dec_mask)
-        rounded = probs.astype(BF)
-        mxs[:, head(i)] = nn(rounded, v).astype(BF)
-        grad_values = tn(rounded, ct)
-        grad_probs = nt(ct, v)
-        grad_scores = probs * (grad_probs - jnp.sum(grad_probs * probs, axis=-1, keepdims=True))
-        grad_keys = tn(grad_scores.astype(BF), q) * SCALE
+    heads = range(HEADS)
+    q = [dq[:, head(i)] for i in heads]
+    k = [nkv[:, head(i)] for i in heads]
+    v = [nkv[:, head(i, True)] for i in heads]
+    ct = [cot[:, mine_head(i)] for i in heads]
+    scores = [nt(q[i], k[i]) for i in heads]
+    grad_probs = [nt(ct[i], v[i]) for i in heads]
+    probs = [softmax(scores[i], dec_mask) for i in heads]
+    rounded = [probs[i].astype(BF) for i in heads]
+    grad_scores = [
+        (probs[i] * (grad_probs[i] - jnp.sum(grad_probs[i] * probs[i], axis=-1, keepdims=True))).astype(BF)
+        for i in heads
+    ]
+    grad_values = [tn(rounded[i], ct[i]) for i in heads]
+    grad_keys = [tn(grad_scores[i], q[i]) * SCALE for i in heads]
+    for i in heads:
+        g2[:, head(i)] = grad_keys[i].astype(BF)
+        g2[:, head(i, True)] = grad_values[i].astype(BF)
+    for i in heads:
+        mxs[:, head(i)] = nn(rounded[i], v[i]).astype(BF)
         rowdot = rowdot + jnp.sum(
-            grad_keys * k.astype(F32) + grad_values * v.astype(F32), axis=1, keepdims=True
+            grad_keys[i] * k[i].astype(F32) + grad_values[i] * v[i].astype(F32), axis=1, keepdims=True
         )
-        g2[:, head(i)] = grad_keys.astype(BF)
-        g2[:, head(i, True)] = grad_values.astype(BF)
     mx_copy = comm.copy(mx_slot, mxs, mxr, partner)
 
     rd[y] = as_row(rowdot)
@@ -514,76 +540,105 @@
 
     def back_enc(r, h):
         b = mod4(y + r) * 2 + h
-        rows = pl.ds(pl.multiple_of(b * HALF, HALF), HALF)
-        pb[b] = nt(g2[...], w[0, rows, :]).astype(BF)
-
-    def scatter_of(h, j):
+        pb[b] = nt(g2[...], w[0, b // 2, pl.ds((b % 2) * 2, 2)].reshape(HALF, COLS)).astype(BF)
+
+    LOW = ROWS // 2
+
+    def part_of(r, h, low):
+        return pb.at[mod4(y + r) * 2 + h, pl.ds(LOW if low else 0, LOW), :]
+
+    def scatter_of(h, low, j):
         return Scatter(
             comm,
-            lambda r: pb.at[mod4(y + r) * 2 + h],
+            lambda r: part_of(r, h, low),
             (rba.at[j, 0], rba.at[j, 1], rbb.at[j, 0], rbb.at[j, 1]),
-            yp, ym, ROWS,
+            yp, ym, LOW,
         )
 
-    away, home = scatter_of(1 - g, 0), scatter_of(g, 1)
+    away, home, low = scatter_of(1 - g, False, 0), scatter_of(g, False, 1), scatter_of(g, True, 2)
+    low_slot = comm.alloc(4)
+
+    def lower(i, r):
+        comm.send(low_slot + i, part_of(r, 1 - g, True), lz.at[i], partner)
+
+    def lower_add(i, r):
+        comm.recv(low_slot + i, lz.at[i], partner)
+        a = part_of(r, g, True)
+        a[...] = (a[...].astype(F32) + lz[i].astype(F32)).astype(BF)
+
     back_enc(2, 1 - g)
     away.first()
+    lower(0, 2)
     back_enc(1, 1 - g)
+    lower(1, 1)
     back_enc(-1, 1 - g)
+    lower(2, -1)
     away.second()
     back_enc(2, g)
     home.first()
+    back_enc(0, 1 - g)
+    lower(3, 0)
     back_enc(1, g)
     back_enc(-1, g)
     away.third()
     home.second()
+    small_wait(rd, rd_base)
+    rdp[0] = rd[0] + rd[1] + rd[2] + rd[3]
+    comm.send(rd_base + 3, rdp.at[0], rdp.at[1], partner)
+    back_enc(0, g)
+    lower_add(0, 2)
+    low.first()
+    home.third()
+    ysum[...] = away.total().astype(BF)
+    r3_slot = comm.alloc(1)
+    comm.send(r3_slot, ysum, r3, partner)
+    lower_add(1, 1)
+    lower_add(2, -1)
+    low.second()
+    low.third()
 
     @pl.when(g == 1)
     def _():
         mx_copy.start()
 
-    back_enc(0, 1 - g)
-    back_enc(0, g)
-    small_wait(rd, rd_base)
-    rdp[0] = rd[0] + rd[1] + rd[2] + rd[3]
-    comm.send(rd_base + 3, rdp.at[0], rdp.at[1], partner)
-    ysum[...] = away.total().astype(BF)
-    r3_slot = comm.alloc(1)
-    comm.send(r3_slot, ysum, r3, partner)
-    home.third()
-    grad_in = home.total()
     comm.recv(rd_base + 3, rdp.at[1], partner)
     dot_all = as_col(rdp[0] + rdp[1])
+    lower_add(3, 0)
+    upper_in = home.total()
     comm.recv(r3_slot, r3, partner)
-    grad_in = grad_in + r3[...].astype(F32)
+    grad_in = jnp.concatenate([upper_in + r3[...].astype(F32), low.total()], axis=0)
     grad_enc = (
         inv_enc * gb[y, 0, 1:2, mine] * grad_in
         - eb[me8].astype(F32) * (inv_enc * inv_enc * dot_all / FEATURES)
     ).astype(BF)
 
     rowdot1 = jnp.zeros((TOK, 1), F32)
-    for i in range(HEADS):
-        q, k, v = qe[:, head(i)], skv[:, head(i)], skv[:, head(i, True)]
-        go = grad_enc[:, head(i)]
-        probs = pe[i]
-        grad_values = tn(probs.astype(BF), go)
-        grad_probs = nt(go, v)
-        grad_scores = probs * (grad_probs - jnp.sum(grad_probs * probs, axis=-1, keepdims=True))
-        grad_keys = tn(grad_scores.astype(BF), q) * SCALE
+    q = [qe[:, head(i)] for i in heads]
+    k = [skv[:, head(i)] for i in heads]
+    v = [skv[:, head(i, True)] for i in heads]
+    go = [grad_enc[:, head(i)] for i in heads]
+    probs = [pe[i] for i in heads]
+    grad_probs = [nt(go[i], v[i]) for i in heads]
+    grad_values = [tn(probs[i].astype(BF), go[i]) for i in heads]
+    grad_scores = [
+        (probs[i] * (grad_probs[i] - jnp.sum(grad_probs[i] * probs[i], axis=-1, keepdims=True))).astype(BF)
+        for i in heads
+    ]
+    grad_keys = [tn(grad_scores[i], q[i]) * SCALE for i in heads]
+    for i in heads:
+        g1[:, head(i)] = grad_keys[i].astype(BF)
+        g1[:, head(i, True)] = grad_values[i].astype(BF)
+    for i in heads:
         rowdot1 = rowdot1 + jnp.sum(
-            grad_keys * k.astype(F32) + grad_values * v.astype(F32), axis=1, keepdims=True
+            grad_keys[i] * k[i].astype(F32) + grad_values[i] * v[i].astype(F32), axis=1, keepdims=True
         )
-        g1[:, head(i)] = grad_keys.astype(BF)
-        g1[:, head(i, True)] = grad_values.astype(BF)
-
     rd1[y] = as_row(rowdot1)
     rd1_base = comm.alloc(4)
     small_start(rd1, rd1_base)
 
     def back_state(r, h):
         b = mod4(y + r) * 2 + h
-        rows = pl.ds(pl.multiple_of(b * HALF, HALF), HALF)
-        pb1[b] = nt(g1[...], w[1, rows, :]).astype(BF)
+        pb1[b] = nt(g1[...], w[1, b // 2, pl.ds((b % 2) * 2, 2)].reshape(HALF, COLS)).astype(BF)
 
     def scatter_state(h):
         return Scatter(
@@ -642,11 +697,11 @@
         mx_copy.wait_send()
 
     comm.drain()
-    either(lambda grp: [make().wait_send() for make in zsent[grp]] and None)
+    either(lambda grp: ([make().wait_send() for make in zsent[grp]], None)[1])
 
 
 def per_device(states, neighbours, cotangent, span_of, counts, kv_weight, gains):
-    keys, values = kv_weight[0, :, 0, :], kv_weight[0, :, 1, :]
+    wide = kv_weight.reshape(TOK, 2 * COLS)
     vmem, smem, hbm = (
         pl.BlockSpec(memory_space=m) for m in (pltpu.VMEM, pltpu.SMEM, pl.ANY)
     )
@@ -658,7 +713,7 @@
         return pltpu.VMEM(shape, F32)
 
     scratch = [
-        bf(2, FEATURES, COLS),
+        bf(2, 4, 4, 2, TOK, COLS),
         bf(TOK, COLS),
         bf(TOK, COLS),
         bf(ROWS, COLS),
@@ -678,10 +733,11 @@
         bf(TOK, HALF),
         bf(ROWS, COLS),
         bf(8, ROWS, HALF),
-        bf(2, 2, ROWS // 2, HALF),
-        bf(2, 2, ROWS, HALF),
-        bf(ROWS, HALF),
-        bf(ROWS, HALF),
+        bf(4, ROWS // 2, HALF),
+        bf(3, 2, ROWS // 4, HALF),
+        bf(3, 2, ROWS // 2, HALF),
+        bf(ROWS // 2, HALF),
+        bf(ROWS // 2, HALF),
         bf(TOK, COLS),
         bf(8, TOK, HALF),
         bf(2, 2, TOK // 2, HALF),
@@ -701,7 +757,7 @@
     result = pl.pallas_call(
         kernel,
         out_shape=jax.ShapeDtypeStruct((TOK, COLS), F32),
-        in_specs=[hbm, hbm, hbm, hbm, hbm, smem, smem, vmem],
+        in_specs=[hbm, hbm, hbm, hbm, smem, smem, vmem],
         out_specs=vmem,
         scratch_shapes=scratch,
         compiler_params=pltpu.CompilerParams(
@@ -709,8 +765,7 @@
         ),
         name="spanned_attention",
     )(
-        keys,
-        values,
+        wide,
         states,
         neighbours.reshape(ROWS, COLS),
         cotangent,

time: 146 us -> 135 us (0.925)
  Pallas kernels: 140 us -> 130 us
    pallas_call x1, Pallas kernels: 140 us -> 130 us  [per_device(): pl.pallas_call(kernel, out_shape=jax.ShapeDtypeStruct((TOK, COLS), F32),...]
    slice x1 -> x0, local copies, waits for them, and re-layouts: 2.1 us -> none  [per_device(): keys, values = (kv_weight[0, :, 0, :], kv_weight[0, :, 1, :])]
    unnamed x1 -> x2, local copies, waits for them, and re-layouts: 1.89 us -> 3.84 us
where the time goes in v3:
time: 135 us; the launch traced here: 134 us
  Pallas kernels  130 us (96%)
  local copies, waits for them, and re-layouts  3.84 us (3%)
    pallas_call x1, Pallas kernels, per_device(): pl.pallas_call(kernel, out_shape=jax.ShapeDtypeStruct((TOK, COLS), F32),...  130 us
    unnamed x2, local copies, waits for them, and re-layouts  3.84 us

profile of v3, /device:TPU:2, one launch (start us, length us, event | category | flops | bytes accessed | tf_op | source)
XLA Modules:
  0.0 134.2 jit_solution(12149382402981920845)
XLA Ops:
  0.7 2.0 %copy.8 = bf16[16,8,2,1024]{3,1,2,0:T(8,128)(2,1)} copy(bf16[16,8,2,1024]{3,2,1,0:T(2,128)(2,1)} %bitcast.8) | data formatting | bytes 1048576
  2.6 129.7 %spanned_attention.1 = f32[128,1024]{1,0:T(8,128)} custom-call(bf16[128,2048]{1,0:T(8,128)(2,1)} %bitcast.7, bf16[128,1024]{1,0:T(8,128)(2,1)} %states_in.1, bf16[256,1024]{1,0:T(8,128)(2,1)} %bitcast.9, bf16[128,1024]{1,0:T(8,128)(2,1)} %cot_in.1, s32[4]{0:T(128)} %span.1, s32[1]{0:T(128)S(6)} %copy.10.counts, f32[2,1024]{1,0:T(2,128)} %bitcast.10), custom_call_target="tpu_custom_call" | custom-call | tf_op jit(solution)/shard_map/spanned_attention/pallas_call | solution.py:757
  132.3 1.9 %copy.11 = f32[1,128,1024]{2,1,0:T(8,128)} copy(f32[1,128,1024]{2,1,0:T(8,128)} %bitcast.6) | data formatting | bytes 1048576

commit v4 on v3

--- a/solution.py
+++ b/solution.py
@@ -22,6 +22,8 @@
 F32 = jnp.float32
 SEMS = 320
 AROWS = TOK
+LOW = 96
+LOW1 = 32
 SPLIT = 64
 
 
@@ -148,7 +150,7 @@
 def kernel(
     wide, states_in, neigh_in, cot_in, span, counts, gains, out,
     w, theirs, states, neigh, cot, sx, xn, gb, ns, eb, en, acc1, skv, qe, pe, acc2, nkv, dq, g2, pb, lz, rba, rbb, r3, ysum,
-    g1, pb1, rca, rcb, t3, ysum1, rd, rdp, rd1, rdp1, mxs, mxr,
+    g1, pb1, lz1, rca, rcb, t3, ysum1, rd, rdp, rd1, rdp1, mxs, mxr,
     ssem, rsem, lsem,
 ):
     g = lax.axis_index("group")
@@ -454,30 +456,34 @@
     ring_own.start()
     slots[5].forward()
     slots[6].start()
+    ring_own.forward()
+    slots[5].rest()
     comm.recv(e_slot, eb.at[y * 2 + 1 - g], partner)
     ring_other.start()
-    ring_own.forward()
-    slots[5].rest()
     ring_own.near()
     relay(1, 1)
     relay(2, -1)
     slots[6].forward()
     slots[7].start()
-    ring_other.forward()
     ring_own.far()
     relay(3, 2)
+
+    def squares(first):
+        def add(i, carry):
+            v = eb[i * 2 + first].astype(F32)
+            return carry + jnp.sum(v * v, axis=1, keepdims=True)
+
+        return lax.fori_loop(0, 4, add, jnp.zeros((ROWS, 1), F32))
+
+    enc_sum = squares(g)
+    ring_other.forward()
     slots[6].rest()
     ring_other.near()
     ring_other.far()
     slots[7].forward()
     for i, r in ((1, 1), (2, -1), (3, 2)):
         comm.recv(e_slot + i, elow(r, 1 - g), partner)
-
-    def esum(i, carry):
-        v = eb[i].astype(F32)
-        return carry + jnp.sum(v * v, axis=1, keepdims=True)
-
-    inv_enc = lax.rsqrt(lax.fori_loop(0, 8, esum, jnp.zeros((ROWS, 1), F32)) / FEATURES + EPSILON)
+    inv_enc = lax.rsqrt((enc_sum + squares(1 - g)) / FEATURES + EPSILON)
 
     for h in range(2):
 
@@ -542,18 +548,17 @@
         b = mod4(y + r) * 2 + h
         pb[b] = nt(g2[...], w[0, b // 2, pl.ds((b % 2) * 2, 2)].reshape(HALF, COLS)).astype(BF)
 
-    LOW = ROWS // 2
+    def rows_of(low):
+        return pl.ds(ROWS - LOW, LOW) if low else pl.ds(0, ROWS - LOW)
 
     def part_of(r, h, low):
-        return pb.at[mod4(y + r) * 2 + h, pl.ds(LOW if low else 0, LOW), :]
+        return pb.at[mod4(y + r) * 2 + h, rows_of(low), :]
 
     def scatter_of(h, low, j):
-        return Scatter(
-            comm,
-            lambda r: part_of(r, h, low),
-            (rba.at[j, 0], rba.at[j, 1], rbb.at[j, 0], rbb.at[j, 1]),
-            yp, ym, LOW,
-        )
+        n = LOW if low else ROWS - LOW
+        short, whole_rows = pl.ds(0, n // 2), pl.ds(0, n)
+        bufs = [rba.at[j, k, short, :] for k in (0, 1)] + [rbb.at[j, k, whole_rows, :] for k in (0, 1)]
+        return Scatter(comm, lambda r: part_of(r, h, low), bufs, yp, ym, n)
 
     away, home, low = scatter_of(1 - g, False, 0), scatter_of(g, False, 1), scatter_of(g, True, 2)
     low_slot = comm.alloc(4)
@@ -640,37 +645,72 @@
         b = mod4(y + r) * 2 + h
         pb1[b] = nt(g1[...], w[1, b // 2, pl.ds((b % 2) * 2, 2)].reshape(HALF, COLS)).astype(BF)
 
-    def scatter_state(h):
-        return Scatter(
-            comm,
-            lambda r: pb1.at[mod4(y + r) * 2 + h],
-            (rca.at[h, 0], rca.at[h, 1], rcb.at[h, 0], rcb.at[h, 1]),
-            yp, ym, TOK,
-        )
-
-    sc = [scatter_state(0), scatter_state(1)]
+    def token_part(r, h, low):
+        rows = pl.ds(TOK - LOW1, LOW1) if low else pl.ds(0, TOK - LOW1)
+        return pb1.at[mod4(y + r) * 2 + h, rows, :]
+
+    def scatter_state(h, low):
+        n, j = (LOW1 if low else TOK - LOW1), h * 2 + low
+        short, whole_rows = pl.ds(0, n // 2), pl.ds(0, n)
+        bufs = [rca.at[j, k, short, :] for k in (0, 1)] + [rcb.at[j, k, whole_rows, :] for k in (0, 1)]
+        return Scatter(comm, lambda r: token_part(r, h, low), bufs, yp, ym, n)
+
+    ups = [scatter_state(h, False) for h in range(2)]
+    lows = [scatter_state(h, True) for h in range(2)]
+    raw_slot = comm.alloc(8)
+    raw = {}
+
+    def raw_send(r, h):
+        i = h * 4 + r % 4
+        raw[r, h] = comm.copy(raw_slot + i, token_part(r, h, True), lz1.at[i], partner)
+        pl.when(g == 0)(lambda: raw[r, h].start())
+
+    def raw_add(*pairs):
+        @pl.when(g == 1)
+        def _():
+            for r, h in pairs:
+                raw[r, h].wait_recv()
+                a = token_part(r, h, True)
+                a[...] = (a[...].astype(F32) + lz1[h * 4 + r % 4].astype(F32)).astype(BF)
+
     for h in range(2):
         back_state(2, h)
-        sc[h].first()
+        ups[h].first()
+        raw_send(2, h)
         back_state(1, h)
         back_state(-1, h)
-        sc[h].second()
-    sc[0].third()
-    back_state(0, 0)
-    back_state(0, 1)
-    sc[1].third()
+        ups[h].second()
+        raw_send(1, h)
+        raw_send(-1, h)
+    for h in range(2):
+        back_state(0, h)
+        raw_send(0, h)
+    ups[0].third()
+    raw_add((2, 0), (2, 1))
+    lows[0].first()
+    lows[1].first()
+    ups[1].third()
     small_wait(rd1, rd1_base)
     rdp1[0] = rd1[0] + rd1[1] + rd1[2] + rd1[3]
     comm.send(rd1_base + 3, rdp1.at[0], rdp1.at[1], partner)
+    raw_add((1, 0), (-1, 0), (1, 1), (-1, 1))
+    for h in range(2):
+        lows[h].second()
     t3_slot = comm.alloc(2)
     t3_copies = [comm.copy(t3_slot + h, ysum1.at[h], t3.at[h], partner) for h in range(2)]
     for h in range(2):
-        ysum1[h] = sc[h].total().astype(BF)
+        ysum1[h] = ups[h].total().astype(BF)
 
         @pl.when(g == 0)
         def _(h=h):
             t3_copies[h].start()
-
+            for r in (1, -1):
+                raw[r, h].wait_send()
+
+        lows[h].third()
+
+    raw_add((0, 0), (0, 1))
+    low_sums = [lows[h].total() for h in range(2)]
     comm.recv(rd1_base + 3, rdp1.at[1], partner)
 
     @pl.when(g == 0)
@@ -680,7 +720,7 @@
             heads_out = mxr if h == 1 else mxs
             cols = slice(h * HALF, (h + 1) * HALF)
             out[:, cols] = states[:, cols].astype(F32) + heads_out[...].astype(F32)
-        for copy in t3_copies:
+        for copy in (*t3_copies, *(raw[r, h] for h in range(2) for r in (2, 0))):
             copy.wait_send()
 
     @pl.when(g == 1)
@@ -690,7 +730,8 @@
         for h in range(2):
             t3_copies[h].wait_recv()
             cols = slice(h * HALF, (h + 1) * HALF)
-            total = ysum1[h].astype(F32) + t3[h].astype(F32)
+            upper = ysum1[h].astype(F32) + t3[h].astype(F32)
+            total = jnp.concatenate([upper, low_sums[h]], axis=0)
             out[:, cols] = (
                 inv_state * gb[y, 1, 0:1, cols] * total - states[:, cols].astype(F32) * factor
             )
@@ -733,17 +774,18 @@
         bf(TOK, HALF),
         bf(ROWS, COLS),
         bf(8, ROWS, HALF),
-        bf(4, ROWS // 2, HALF),
-        bf(3, 2, ROWS // 4, HALF),
-        bf(3, 2, ROWS // 2, HALF),
-        bf(ROWS // 2, HALF),
-        bf(ROWS // 2, HALF),
+        bf(4, LOW, HALF),
+        bf(3, 2, (ROWS - LOW) // 2, HALF),
+        bf(3, 2, ROWS - LOW, HALF),
+        bf(ROWS - LOW, HALF),
+        bf(ROWS - LOW, HALF),
         bf(TOK, COLS),
         bf(8, TOK, HALF),
-        bf(2, 2, TOK // 2, HALF),
-        bf(2, 2, TOK, HALF),
-        bf(2, TOK, HALF),
-        bf(2, TOK, HALF),
+        bf(8, LOW1, HALF),
+        bf(4, 2, (TOK - LOW1) // 2, HALF),
+        bf(4, 2, TOK - LOW1, HALF),
+        bf(2, TOK - LOW1, HALF),
+        bf(2, TOK - LOW1, HALF),
         f32(4, 8, ROWS),
         f32(2, 8, ROWS),
         f32(4, 8, TOK),

time: 135 us -> 131 us (0.970)
  Pallas kernels: 130 us -> 126 us
    pallas_call x1, Pallas kernels: 130 us -> 126 us  [per_device(): pl.pallas_call(kernel, out_shape=jax.ShapeDtypeStruct((TOK, COLS), F32),...]
where the time goes in v4:
time: 131 us
  Pallas kernels  126 us (96%)
  local copies, waits for them, and re-layouts  3.84 us (3%)
    pallas_call x1, Pallas kernels, per_device(): pl.pallas_call(kernel, out_shape=jax.ShapeDtypeStruct((TOK, COLS), F32),...  126 us
    unnamed x2, local copies, waits for them, and re-layouts  3.84 us

profile of v4, /device:TPU:2, one launch (start us, length us, event | category | flops | bytes accessed | tf_op | source)
XLA Modules:
  0.0 130.6 jit_solution(8711356869111723712)
XLA Ops:
  0.7 2.0 %copy.8 = bf16[16,8,2,1024]{3,1,2,0:T(8,128)(2,1)} copy(bf16[16,8,2,1024]{3,2,1,0:T(2,128)(2,1)} %bitcast.8) | data formatting | bytes 1048576
  2.6 126.1 %spanned_attention.1 = f32[128,1024]{1,0:T(8,128)} custom-call(bf16[128,2048]{1,0:T(8,128)(2,1)} %bitcast.7, bf16[128,1024]{1,0:T(8,128)(2,1)} %states_in.1, bf16[256,1024]{1,0:T(8,128)(2,1)} %bitcast.9, bf16[128,1024]{1,0:T(8,128)(2,1)} %cot_in.1, s32[4]{0:T(128)} %span.1, s32[1]{0:T(128)S(6)} %copy.10.counts, f32[2,1024]{1,0:T(2,128)} %bitcast.10), custom_call_target="tpu_custom_call" | custom-call | tf_op jit(solution)/shard_map/spanned_attention/pallas_call | solution.py:799
  128.7 1.9 %copy.11 = f32[1,128,1024]{2,1,0:T(8,128)} copy(f32[1,128,1024]{2,1,0:T(8,128)} %bitcast.6) | data formatting | bytes 1048576

commit v5 on v4

--- a/solution.py
+++ b/solution.py
@@ -22,7 +22,9 @@
 F32 = jnp.float32
 SEMS = 320
 AROWS = TOK
-LOW = 96
+FAR_BY_Z = (4,)
+UP = 160
+LOW = 128
 LOW1 = 32
 SPLIT = 64
 
@@ -285,9 +287,11 @@
     class Slot:
         def __init__(self, s):
             (m0, r0), (m1, r1) = plan(0, s), plan(1, s)
+            self.m_, self.arrival = PLAN[0][s]
             self.s, self.m, self.rz = s, m0 + (m1 - m0) * g, r0 + (r1 - r0) * g
             self.ring = Ring(comm, self.half, xp, xm)
             self.sib = comm.alloc(4)
+            self.far = comm.alloc(2)
 
         def half(self, r, k):
             return main_half(self.m, r, self.rz, k)
@@ -303,13 +307,27 @@
             self.share(0)
 
         def forward(self):
-            self.ring.forward()
+            if self.s not in FAR_BY_Z:
+                self.ring.forward()
 
         def rest(self):
+            if self.s in FAR_BY_Z:
+                comm.recv(self.ring.base, self.half(-1, 0), xm)
+                comm.recv(self.ring.base + 2, self.half(1, 1), xp)
             self.ring.near()
             self.share(-1, 1)
-            self.ring.far()
+            if self.s in FAR_BY_Z:
+                comm.recv(self.far, self.half(2, 0), zm)
+                comm.recv(self.far + 1, self.half(2, 1), zp)
+            else:
+                self.ring.far()
             self.share(2)
+
+        def pass_far(self, to):
+            if to.s in FAR_BY_Z:
+                k, dev = (0, zp) if ORDER[to.m_][self.arrival] == -1 else (1, zm)
+                ref = self.half(2, k)
+                comm.send(to.far + k, ref, ref, dev)
 
     slots = [Slot(s) for s in range(8)]
     sib_first = slots[0].sib
@@ -393,9 +411,11 @@
     slots[3].start()
     pl.when(g == 0)(lambda: zout(0))
     slots[2].rest()
+    slots[2].pass_far(slots[4])
     slots[3].forward()
     slots[4].start()
     slots[3].rest()
+    slots[3].pass_far(slots[4])
     slots[4].forward()
     slots[5].start()
     project_states(0)
@@ -423,8 +443,8 @@
     def softmax(scores, mask):
         scores = jnp.where(mask, scores * SCALE, NEG_LARGE)
         top = jnp.max(scores, axis=-1, keepdims=True)
-        raised = jnp.where(mask, jnp.exp(scores - top), 0.0)
-        return raised / jnp.sum(raised, axis=-1, keepdims=True)
+        raised = jnp.exp(scores - top)
+        return raised * (1.0 / jnp.sum(raised, axis=-1, keepdims=True))
 
     def head(i, second=False):
         start = i * HD + (HALF if second else 0)
@@ -443,56 +463,53 @@
     def ehalf(grp, rows):
         return lambda r, k: eb.at[mod4(y + r) * 2 + grp, pl.ds(k * rows, rows), :]
 
-    def elow(r, grp):
-        return eb.at[mod4(y + r) * 2 + grp, pl.ds(128, 128), :]
-
-    e_slot = comm.alloc(4)
+    def epart(r, grp, low):
+        rows = pl.ds(UP, ROWS - UP) if low else pl.ds(0, UP)
+        return eb.at[mod4(y + r) * 2 + grp, rows, :]
+
+    e_slot = comm.alloc(5)
 
     def relay(i, r):
-        comm.send(e_slot + i, elow(r, g), elow(r, g), partner)
-
-    comm.send(e_slot, eb.at[me8], eb.at[me8], partner)
-    ring_own, ring_other = Ring(comm, ehalf(g, 128), yp, ym), Ring(comm, ehalf(1 - g, 64), yp, ym)
+        comm.send(e_slot + i, epart(r, g, True), epart(r, g, True), partner)
+
+    comm.send(e_slot, epart(0, g, False), epart(0, g, False), partner)
+    ring_own, ring_other = Ring(comm, ehalf(g, 128), yp, ym), Ring(comm, ehalf(1 - g, UP // 2), yp, ym)
     ring_own.start()
+    relay(4, 0)
     slots[5].forward()
     slots[6].start()
     ring_own.forward()
+    comm.recv(e_slot, epart(0, 1 - g, False), partner)
+    ring_other.start()
     slots[5].rest()
-    comm.recv(e_slot, eb.at[y * 2 + 1 - g], partner)
-    ring_other.start()
+    slots[5].pass_far(slots[7])
     ring_own.near()
     relay(1, 1)
     relay(2, -1)
     slots[6].forward()
     slots[7].start()
+    ring_other.forward()
     ring_own.far()
     relay(3, 2)
 
-    def squares(first):
-        def add(i, carry):
-            v = eb[i * 2 + first].astype(F32)
+    def scaled(h):
+        def step(i, carry):
+            v = eb[i * 2 + h].astype(F32)
+            cols = pl.ds(pl.multiple_of(h * HALF, HALF), HALF)
+            en[i * 2 + h] = (v * gb[i, 0, 1:2, cols]).astype(BF)
             return carry + jnp.sum(v * v, axis=1, keepdims=True)
 
-        return lax.fori_loop(0, 4, add, jnp.zeros((ROWS, 1), F32))
-
-    enc_sum = squares(g)
-    ring_other.forward()
+        return lax.fori_loop(0, 4, step, jnp.zeros((ROWS, 1), F32))
+
+    enc_sum = scaled(g)
     slots[6].rest()
+    slots[6].pass_far(slots[7])
     ring_other.near()
     ring_other.far()
     slots[7].forward()
-    for i, r in ((1, 1), (2, -1), (3, 2)):
-        comm.recv(e_slot + i, elow(r, 1 - g), partner)
-    inv_enc = lax.rsqrt((enc_sum + squares(1 - g)) / FEATURES + EPSILON)
-
-    for h in range(2):
-
-        def norm_enc(i, carry, h=h):
-            gain = gb[i, 0, 1:2, h * HALF : (h + 1) * HALF]
-            en[i * 2 + h] = (eb[i * 2 + h].astype(F32) * inv_enc * gain).astype(BF)
-            return carry
-
-        lax.fori_loop(0, 4, norm_enc, 0)
+    for i, r in ((4, 0), (1, 1), (2, -1), (3, 2)):
+        comm.recv(e_slot + i, epart(r, 1 - g, True), partner)
+    inv_enc = lax.rsqrt((enc_sum + scaled(1 - g)) / FEATURES + EPSILON)
 
     acc2[...] = jnp.zeros_like(acc2)
 
@@ -511,7 +528,7 @@
         project_enc(i)
     slots[7].rest()
     project_enc(3)
-    nkv[...] = acc2[...].astype(BF)
+    nkv[...] = (acc2[...] * inv_enc).astype(BF)
 
     mx_slot = comm.alloc(1)
     rowdot = jnp.zeros((ROWS, 1), F32)
@@ -533,17 +550,6 @@
     for i in heads:
         g2[:, head(i)] = grad_keys[i].astype(BF)
         g2[:, head(i, True)] = grad_values[i].astype(BF)
-    for i in heads:
-        mxs[:, head(i)] = nn(rounded[i], v[i]).astype(BF)
-        rowdot = rowdot + jnp.sum(
-            grad_keys[i] * k[i].astype(F32) + grad_values[i] * v[i].astype(F32), axis=1, keepdims=True
-        )
-    mx_copy = comm.copy(mx_slot, mxs, mxr, partner)
-
-    rd[y] = as_row(rowdot)
-    rd_base = comm.alloc(4)
-    small_start(rd, rd_base)
-
     def back_enc(r, h):
         b = mod4(y + r) * 2 + h
         pb[b] = nt(g2[...], w[0, b // 2, pl.ds((b % 2) * 2, 2)].reshape(HALF, COLS)).astype(BF)
@@ -579,6 +585,17 @@
     back_enc(-1, 1 - g)
     lower(2, -1)
     away.second()
+    for i in heads:
+        mxs[:, head(i)] = nn(rounded[i], v[i]).astype(BF)
+        rowdot = rowdot + jnp.sum(
+            grad_keys[i] * k[i].astype(F32) + grad_values[i] * v[i].astype(F32), axis=1, keepdims=True
+        )
+    mx_copy = comm.copy(mx_slot, mxs, mxr, partner)
+
+    rd[y] = as_row(rowdot)
+    rd_base = comm.alloc(4)
+    small_start(rd, rd_base)
+
     back_enc(2, g)
     home.first()
     back_enc(0, 1 - g)
@@ -633,14 +650,6 @@
     for i in heads:
         g1[:, head(i)] = grad_keys[i].astype(BF)
         g1[:, head(i, True)] = grad_values[i].astype(BF)
-    for i in heads:
-        rowdot1 = rowdot1 + jnp.sum(
-            grad_keys[i] * k[i].astype(F32) + grad_values[i] * v[i].astype(F32), axis=1, keepdims=True
-        )
-    rd1[y] = as_row(rowdot1)
-    rd1_base = comm.alloc(4)
-    small_start(rd1, rd1_base)
-
     def back_state(r, h):
         b = mod4(y + r) * 2 + h
         pb1[b] = nt(g1[...], w[1, b // 2, pl.ds((b % 2) * 2, 2)].reshape(HALF, COLS)).astype(BF)
@@ -685,6 +694,14 @@
     for h in range(2):
         back_state(0, h)
         raw_send(0, h)
+    for i in heads:
+        rowdot1 = rowdot1 + jnp.sum(
+            grad_keys[i] * k[i].astype(F32) + grad_values[i] * v[i].astype(F32), axis=1, keepdims=True
+        )
+    rd1[y] = as_row(rowdot1)
+    rd1_base = comm.alloc(4)
+    small_start(rd1, rd1_base)
+
     ups[0].third()
     raw_add((2, 0), (2, 1))
     lows[0].first()

time: 131 us -> 128 us (0.977)
  Pallas kernels: 126 us -> 124 us
    pallas_call x1, Pallas kernels: 126 us -> 124 us  [per_device(): pl.pallas_call(kernel, out_shape=jax.ShapeDtypeStruct((TOK, COLS), F32),...]
where the time goes in v5:
time: 128 us
  Pallas kernels  124 us (97%)
  local copies, waits for them, and re-layouts  3.84 us (3%)
    pallas_call x1, Pallas kernels, per_device(): pl.pallas_call(kernel, out_shape=jax.ShapeDtypeStruct((TOK, COLS), F32),...  124 us
    unnamed x2, local copies, waits for them, and re-layouts  3.84 us

profile of v5, /device:TPU:2, one launch (start us, length us, event | category | flops | bytes accessed | tf_op | source)
XLA Modules:
  0.0 128.2 jit_solution(3512198864586083594)
XLA Ops:
  0.7 2.0 %copy.8 = bf16[16,8,2,1024]{3,1,2,0:T(8,128)(2,1)} copy(bf16[16,8,2,1024]{3,2,1,0:T(2,128)(2,1)} %bitcast.8) | data formatting | bytes 1048576
  2.6 123.7 %spanned_attention.1 = f32[128,1024]{1,0:T(8,128)} custom-call(bf16[128,2048]{1,0:T(8,128)(2,1)} %bitcast.7, bf16[128,1024]{1,0:T(8,128)(2,1)} %states_in.1, bf16[256,1024]{1,0:T(8,128)(2,1)} %bitcast.9, bf16[128,1024]{1,0:T(8,128)(2,1)} %cot_in.1, s32[4]{0:T(128)} %span.1, s32[1]{0:T(128)S(6)} %copy.10.counts, f32[2,1024]{1,0:T(2,128)} %bitcast.10), custom_call_target="tpu_custom_call" | custom-call | tf_op jit(solution)/shard_map/spanned_attention/pallas_call | solution.py:816
  126.3 1.9 %copy.11 = f32[1,128,1024]{2,1,0:T(8,128)} copy(f32[1,128,1024]{2,1,0:T(8,128)} %bitcast.6) | data formatting | bytes 1048576

commit v6 on v5

--- a/solution.py
+++ b/solution.py
@@ -408,8 +408,8 @@
     acc1[...] = jnp.zeros_like(acc1)
     slots[1].rest()
     slots[2].forward()
+    pl.when(g == 0)(lambda: zout(0))
     slots[3].start()
-    pl.when(g == 0)(lambda: zout(0))
     slots[2].rest()
     slots[2].pass_far(slots[4])
     slots[3].forward()
@@ -736,7 +736,7 @@
         for h in range(2):
             heads_out = mxr if h == 1 else mxs
             cols = slice(h * HALF, (h + 1) * HALF)
-            out[:, cols] = states[:, cols].astype(F32) + heads_out[...].astype(F32)
+            out[:, cols] = (states[:, cols].astype(F32) + heads_out[...].astype(F32)).astype(BF)
         for copy in (*t3_copies, *(raw[r, h] for h in range(2) for r in (2, 0))):
             copy.wait_send()
 
@@ -751,7 +751,7 @@
             total = jnp.concatenate([upper, low_sums[h]], axis=0)
             out[:, cols] = (
                 inv_state * gb[y, 1, 0:1, cols] * total - states[:, cols].astype(F32) * factor
-            )
+            ).astype(BF)
         mx_copy.wait_send()
 
     comm.drain()
@@ -815,7 +815,7 @@
     ]
     result = pl.pallas_call(
         kernel,
-        out_shape=jax.ShapeDtypeStruct((TOK, COLS), F32),
+        out_shape=jax.ShapeDtypeStruct((TOK, COLS), BF),
         in_specs=[hbm, hbm, hbm, hbm, smem, smem, vmem],
         out_specs=vmem,
         scratch_shapes=scratch,
@@ -832,7 +832,7 @@
         counts,
         gains.reshape(2, COLS),
     )
-    return result[None]
+    return result.astype(F32)[None]
 
 
 def solution(mesh):

time: 128 us -> 128 us (level)
  local copies, waits for them, and re-layouts: 3.84 us -> 1.96 us
  other arithmetic: 0 us -> 1.79 us
    unnamed x2 -> x1, local copies, waits for them, and re-layouts: 3.84 us -> 1.96 us
    broadcast_in_dim x0 -> x1, other arithmetic: none -> 1.79 us  [per_device(): return result.astype(F32)[None]]
where the time goes in v6:
time: 128 us
  Pallas kernels  123 us (96%)
  local copies, waits for them, and re-layouts  1.96 us (2%)
  other arithmetic  1.79 us (1%)
    pallas_call x1, Pallas kernels, per_device(): pl.pallas_call(kernel, out_shape=jax.ShapeDtypeStruct((TOK, COLS), BF), i...  123 us

profile of v6, /device:TPU:2, one launch (start us, length us, event | category | flops | bytes accessed | tf_op | source)
XLA Modules:
  0.0 127.5 jit_solution(10642345625450978685)
XLA Ops:
  0.7 2.0 %copy.8 = bf16[16,8,2,1024]{3,1,2,0:T(8,128)(2,1)} copy(bf16[16,8,2,1024]{3,2,1,0:T(2,128)(2,1)} %bitcast.10) | data formatting | bytes 1048576
  2.6 123.1 %spanned_attention.1 = bf16[128,1024]{1,0:T(8,128)(2,1)} custom-call(bf16[128,2048]{1,0:T(8,128)(2,1)} %bitcast.8, bf16[128,1024]{1,0:T(8,128)(2,1)} %states_in.1, bf16[256,1024]{1,0:T(8,128)(2,1)} %bitcast.9, bf16[128,1024]{1,0:T(8,128)(2,1)} %cot_in.1, s32[4]{0:T(128)} %span.1, s32[1]{0:T(128)S(6)} %copy.9.counts, f32[2,1024]{1,0:T(2,128)} %bitcast.11), custom_call_target="tpu_custom_call" | custom-call | tf_op jit(solution)/shard_map/spanned_attention/pallas_call | solution.py:816
  125.7 1.8 %bitcast_convert_fusion = f32[1,128,1024]{2,1,0:T(8,128)} fusion(bf16[128,1024]{1,0:T(8,128)(2,1)} %spanned_attention.1), kind=kLoop, calls=%fused_computation | loop fusion | flops 131072 | bytes 786432 | tf_op jit(solution)/shard_map/broadcast_in_dim | solution.py:835
